TPU v7x, 128 devices: a whole 4x4x4 slice. The times are simulated.
128 devices in a mesh: seg: 32 (over x, z, core), head: 4 (over y).
Axes of the slice: x: 4, y: 4, z: 4, core: 2. Of those that a mesh axis runs over, the one named last changes fastest.
Arguments:
- token_ids: int32 [4096], P('seg'), may hold values from 0 to 31999
- embed_table: bfloat16 [32000, 2560], P('seg', 'head'), may hold values from -6 to 6
- norm_gains: float32 [2, 2560], replicated, may hold values from 0.1 to 1.9
- query_weight: bfloat16 [2, 2560, 2048], P(None, None, 'head')
- key_weight: bfloat16 [2, 2560, 2048], P(None, None, 'head')
- value_weight: bfloat16 [2, 2560, 2048], P(None, None, 'head'), may hold values from -0.125 to 0.125
- out_weight: bfloat16 [2, 2048, 2560], P(None, 'head'), may hold values from -0.125 to 0.125
Outputs:
- final_states: bfloat16 [4096, 2560], P(('seg', 'head'))
Inputs may be any that keep to these rules, and one draw needn't show every extreme that they name: `token_ids`: token ids of the book span in reading order.
All inputs are finite; a program needn't handle non-finite values.
Results may differ from a plain program's by a relative error of at most 0.04.
Values may be sent and summed in bfloat16 or wider, within the bound.
A program may use at most 128 MiB of HBM per device.

v0:
```python
import jax
import jax.numpy as jnp
from jax import lax
from jax.sharding import PartitionSpec as P

HD = 64
LAYERS = 2


EPSILON = 1e-05


def shifted(value, axis, steps):
    count = lax.axis_size(axis)
    leading, last = (max(0, -steps), min(count, count - steps))
    return lax.ppermute(value, axis, [(source, source + steps) for source in range(leading, last)])


def rotate(field, positions):
    half_dim = field.shape[-1] // 2
    frequency = 10000.0 ** (-jnp.arange(half_dim, dtype=jnp.float32) / half_dim)
    angles = positions.astype(jnp.float32)[:, None] * frequency[None, :]
    cosine = jnp.cos(angles)[:, None, :]
    sine = jnp.sin(angles)[:, None, :]
    front = field[..., :half_dim]
    back = field[..., half_dim:]
    return jnp.concatenate([front * cosine - back * sine, front * sine + back * cosine], axis=-1)


def normalize(states, gain):
    widened = states.astype(jnp.float32)
    mean_square = jnp.mean(widened * widened, axis=-1, keepdims=True)
    return (widened * lax.rsqrt(mean_square + EPSILON) * gain).astype(jnp.bfloat16)


def attend_block(queries, keys_all, values_all, has_memory):
    count = queries.shape[0]
    scores = jnp.einsum(
        "qhd,khd->hqk", queries, keys_all, preferred_element_type=jnp.float32
    ) * queries.shape[-1] ** (-0.5)
    query_place = jnp.arange(count, dtype=jnp.int32)[:, None]
    key_place = jnp.arange(2 * count, dtype=jnp.int32)[None, :]
    allowed = jnp.where(key_place < count, has_memory, key_place - count <= query_place)
    scores = jnp.where(allowed[None], scores, -1e30)
    top_score = jnp.max(scores, axis=-1, keepdims=True)
    weights = jnp.exp(scores - top_score)
    probs = (weights / jnp.sum(weights, axis=-1, keepdims=True)).astype(jnp.bfloat16)
    mixed = jnp.einsum("hqk,khd->qhd", probs, values_all, preferred_element_type=jnp.float32)
    return mixed.astype(jnp.bfloat16).reshape(count, -1)


def body(token_ids, embed_table, norm_gains, query_weight, key_weight, value_weight, out_weight):
    seg_len = token_ids.shape[0]
    head_count = lax.axis_size("head")
    local_heads = query_weight.shape[2] // HD
    book_ids = lax.all_gather(token_ids, "seg", axis=0, tiled=True)
    vocab_rows = embed_table.shape[0]
    seg_index = lax.axis_index("seg")
    vocab_start = seg_index * vocab_rows
    chosen = book_ids - vocab_start
    inside = ((chosen >= 0) & (chosen < vocab_rows)).astype(jnp.float32)
    clamped = jnp.clip(chosen, 0, vocab_rows - 1)
    rows = jnp.take(embed_table, clamped, axis=0).astype(jnp.float32)
    embedded = lax.psum_scatter(
        (rows * inside[:, None]).astype(jnp.bfloat16), "seg", scatter_dimension=0, tiled=True
    )
    states = lax.all_gather(embedded, "head", axis=1, tiled=True)
    positions = seg_index * seg_len + jnp.arange(seg_len, dtype=jnp.int32)
    has_memory = seg_index > 0
    row_count = seg_len // head_count
    row_start = lax.axis_index("head") * row_count

    def project(normed, weight, depth):
        return jnp.dot(normed, weight[depth], preferred_element_type=jnp.float32).reshape(
            seg_len, local_heads, HD
        )

    normed = normalize(states, norm_gains[0])
    residual = states
    for depth in range(LAYERS):
        queries = rotate(project(normed, query_weight, depth), positions).astype(jnp.bfloat16)
        keys_now = rotate(project(normed, key_weight, depth), positions).astype(jnp.bfloat16)
        values_now = project(normed, value_weight, depth).astype(jnp.bfloat16)
        normed_past = shifted(normed, "seg", 1)
        keys_past = rotate(project(normed_past, key_weight, depth), positions - seg_len).astype(
            jnp.bfloat16
        )
        values_past = project(normed_past, value_weight, depth).astype(jnp.bfloat16)
        keys_all = jnp.concatenate([keys_past, keys_now], 0)
        values_all = jnp.concatenate([values_past, values_now], 0)
        mixed = attend_block(queries, keys_all, values_all, has_memory)
        summed = lax.psum(
            jnp.dot(mixed, out_weight[depth], preferred_element_type=jnp.float32), "head"
        )
        residual = (residual.astype(jnp.float32) + summed).astype(jnp.bfloat16)
        if depth + 1 < LAYERS:
            normed = normalize(residual, norm_gains[depth + 1])
    return lax.dynamic_slice_in_dim(residual, row_start, row_count, 0)


def solution(mesh):
    placed = (
        P("seg"),
        P("seg", "head"),
        P(),
        P(None, None, "head"),
        P(None, None, "head"),
        P(None, None, "head"),
        P(None, "head", None),
    )
    return jax.shard_map(
        body, mesh=mesh, in_specs=placed, out_specs=P(("seg", "head"), None), check_vma=False
    )
```

profile of v0, /device:TPU:0, one launch (start us, length us, event | category | flops | bytes accessed | tf_op | source)
XLA Modules:
  0.0 303.4 jit_solution(3967452895826827887)
XLA Ops:
  6.5 22.9 %all-gather = s32[32,1,128]{2,1,0:T(1,128)S(1)} all-gather(s32[1,1,128]{2,1,0:T(1,128)} %bitcast.96), channel_id=1, replica_groups=mesh['seg'=32,'head'=4] {'seg'}, dimensions={0}, use_global_device_ids=true | all-gather | bytes 16896 | tf_op jit(solution)/shard_map/all_gather | solution.py:56
  29.6 17.7 %gather_fusion = bf16[4096,640]{1,0:T(8,128)(2,1)} fusion(bf16[1000,640]{1,0:T(8,128)(2,1)S(1)} %copy-done, s32[4096]{0:T(1024)S(1)} %fusion.71), kind=kCustom, calls=%fused_computation | custom fusion | bytes 10502144 | tf_op jit(solution)/shard_map/jit(_take)/gather | solution.py:63
  47.2 7.2 %multiply_convert_fusion = bf16[4096,640]{1,0:T(8,128)(2,1)} fusion(f32[4096]{0:T(1024)S(1)} %bitcast.95, bf16[4096,640]{1,0:T(8,128)(2,1)} %gather_fusion, pred[4096]{0:T(1024)(128)(4,1)S(1)} %compare_and_fusion), kind=kLoop, calls=%fused_computation.3 | loop fusion | flops 10485760 | bytes 10506240 | tf_op jit(solution)/shard_map/convert_element_type | solution.py:65
  54.5 4.4 %slice_bitcast_fusion.1 = (bf16[512,2560]{0,1:T(8,128)(2,1)}, bf16[512,2560]{0,1:T(8,128)(2,1)S(1)}) fusion(bf16[2,2560,512]{2,1,0:T(8,128)(2,1)} %param.10), kind=kLoop, calls=%fused_computation.10 | loop fusion | bytes 10485760 | tf_op jit(solution)/shard_map/dot_general | solution.py:74
  58.9 2.9 copy.19
  61.8 4.5 %slice_bitcast_fusion.2 = (bf16[512,2560]{0,1:T(8,128)(2,1)S(1)}, bf16[512,2560]{0,1:T(8,128)(2,1)}) fusion(bf16[2,2560,512]{2,1,0:T(8,128)(2,1)} %param.11), kind=kLoop, calls=%fused_computation.12 | loop fusion | bytes 10485760 | tf_op jit(solution)/shard_map/dot_general | solution.py:74
  66.3 2.8 copy.20
  69.1 5.4 %fusion.96 = (bf16[1,2560,512]{2,1,0:T(8,128)(2,1)}, bf16[1,2560,512]{2,1,0:T(8,128)(2,1)}) fusion(bf16[2,2560,512]{2,1,0:T(8,128)(2,1)} %param.12), kind=kLoop, calls=%fused_computation.129 | loop fusion | bytes 10485760 | tf_op jit(solution)/shard_map/slice | solution.py:74
  74.5 3.0 %copy.24 = bf16[1,2560,512]{1,2,0:T(8,128)(2,1)S(1)} copy(bf16[1,2560,512]{2,1,0:T(8,128)(2,1)} %get-tuple-element.10) | data formatting | bytes 5242880
  78.5 60.6 %reduce-scatter.2.cloned.1.call-done = bf16[128,640]{1,0:T(8,128)(2,1)} async-done(((bf16[4096,640]{1,0:T(8,128)(2,1)}), bf16[128,640]{1,0:T(8,128)(2,1)}) %reduce-scatter.2.cloned.1.call-update) | async-done | bytes 163856 | tf_op jit(solution)/shard_map/reduce_scatter | solution.py:64
  139.1 14.5 %all_gather.7 = bf16[128,2560]{1,0:T(8,128)(2,1)S(1)} all-gather(bf16[128,640]{1,0:T(8,128)(2,1)} %reduce-scatter.2.cloned.1.call-done), channel_id=1, replica_groups=mesh['seg'=32,'head'=4] {'head'}, dimensions={1}, use_global_device_ids=true | all-gather | bytes 819200 | tf_op jit(solution)/shard_map/all_gather | solution.py:67
  160.4 2.5 fusion.97
  162.9 2.0 convolution_convert_fusion.5
  165.3 3.5 %fusion.4 = f32[128,2560]{1,0:T(8,128)} fusion(bf16[128,512]{0,1:T(8,128)(2,1)S(1)} %bitcast.93, bf16[2,512,2560]{2,1,0:T(8,128)(2,1)} %param.13), kind=kOutput, calls=%fused_computation.6 | convolution fusion | flops 335544320 | bytes 4063232 | tf_op jit(solution)/shard_map/dot_general | solution.py:93
  168.9 2.8 copy.22
  171.7 4.4 %copy.23 = bf16[512,2560]{1,0:T(8,128)(2,1)} copy(bf16[512,2560]{0,1:T(8,128)(2,1)} %get-tuple-element.14) | data formatting | bytes 5242880 | tf_op jit(solution)/shard_map/dot_general | solution.py:74
  176.1 3.0 copy.25
  179.1 44.3 %all-reduce.3.cloned.1.call-done = f32[128,2560]{1,0:T(8,128)} async-done(((f32[128,2560]{1,0:T(8,128)}), f32[128,2560]{1,0:T(8,128)}) %all-reduce.3.cloned.1.call-update) | async-done | bytes 1310736 | tf_op jit(solution)/shard_map/psum | solution.py:92
  223.4 1.7 multiply_reduce_fusion
  225.4 1.8 collective-permute-start.1
  232.0 2.5 fusion.102
  236.1 3.4 %fusion.2 = f32[128,2560]{1,0:T(8,128)} fusion(bf16[128,512]{0,1:T(8,128)(2,1)S(1)} %bitcast.94, bf16[2,512,2560]{2,1,0:T(8,128)(2,1)} %param.13), kind=kOutput, calls=%fused_computation.4 | convolution fusion | flops 335544320 | bytes 4063232 | tf_op jit(solution)/shard_map/dot_general | solution.py:93
  239.5 55.6 %all-reduce.5.cloned.1.call-done = f32[128,2560]{1,0:T(8,128)} async-done(((f32[128,2560]{1,0:T(8,128)}), f32[128,2560]{1,0:T(8,128)}) %all-reduce.5.cloned.1.call-update) | async-done | bytes 1310736 | tf_op jit(solution)/shard_map/psum | solution.py:92
  295.1 1.8 fusion.35
  (66 shorter events, 14.7 us)
Async XLA Ops:
  6.5 23.0 %copy-start = (bf16[1000,640]{1,0:T(8,128)(2,1)S(1)}, bf16[1000,640]{1,0:T(8,128)(2,1)}, u32[]{:S(2)}) copy-start(bf16[1000,640]{1,0:T(8,128)(2,1)} %param.8) | copy-start | bytes 3840004
  6.5 132.6 %reduce-scatter.2.cloned.1.call-start = ((), (), s32[]{:S(2)}) async-start(), calls=%async_computation.1 | async-start | bytes 5406720 | tf_op jit(solution)/shard_map/reduce_scatter | solution.py:64
  54.4 169.0 %all-reduce.3.cloned.1.call-start = ((), (), s32[]{:S(2)}) async-start(), calls=%async_computation.2 | async-start | bytes 2621440 | tf_op jit(solution)/shard_map/psum | solution.py:92
  74.5 3.1 %copy-start.10 = (f32[2,2560]{1,0:T(2,128)S(1)}, f32[2,2560]{1,0:T(2,128)}, u32[]{:S(2)}) copy-start(f32[2,2560]{1,0:T(2,128)} %param.9) | copy-start | bytes 61444
  139.1 16.5 %copy-start.4 = (bf16[512,2560]{1,0:T(8,128)(2,1)S(1)}, bf16[512,2560]{1,0:T(8,128)(2,1)}, u32[]{:S(2)}) copy-start(bf16[512,2560]{1,0:T(8,128)(2,1)} %copy.19) | copy-start | bytes 7864324
  154.1 2.3 copy-start.2
  154.1 4.7 %collective-permute-start = (bf16[128,2560]{1,0:T(8,128)(2,1)S(1)}, bf16[128,2560]{1,0:T(8,128)(2,1)S(1)}, u32[]{:S(2)}, u32[]{:S(2)}) collective-permute-start(bf16[128,2560]{1,0:T(8,128)(2,1)S(1)} %fusion.16), channel_id=1, source_target_pairs={{0,4},{4,8},{8,12},{12,16},{16,20},{20,24},{24,28},{28,32},{32,36}... | collective-permute-start | bytes 1966088 | tf_op jit(solution)/shard_map/ppermute | solution.py:16
  158.9 1.6 copy-start.8
  162.9 2.0 copy-start.12
  165.3 3.6 %copy-start.6 = (bf16[512,2560]{0,1:T(8,128)(2,1)S(1)}, bf16[512,2560]{0,1:T(8,128)(2,1)}, u32[]{:S(2)}) copy-start(bf16[512,2560]{0,1:T(8,128)(2,1)} %get-tuple-element.11) | copy-start | bytes 7864324
  168.8 126.3 %all-reduce.5.cloned.1.call-start = ((), (), s32[]{:S(2)}) async-start(), calls=%async_computation.3 | async-start | bytes 2621440 | tf_op jit(solution)/shard_map/psum | solution.py:92
  223.4 3.8 %copy-start.5 = (bf16[512,2560]{1,0:T(8,128)(2,1)S(1)}, bf16[512,2560]{1,0:T(8,128)(2,1)}, u32[]{:S(2)}) copy-start(bf16[512,2560]{1,0:T(8,128)(2,1)} %copy.22) | copy-start | bytes 7864324
  225.2 2.8 copy-start.7
  225.4 2.7 copy-start.3
  225.4 5.1 %collective-permute-start.1 = (bf16[128,2560]{1,0:T(8,128)(2,1)S(1)}, bf16[128,2560]{1,0:T(8,128)(2,1)S(1)}, u32[]{:S(2)}, u32[]{:S(2)}) collective-permute-start(bf16[128,2560]{1,0:T(8,128)(2,1)S(1)} %multiply_convert_fusion.1), channel_id=1, source_target_pairs={{0,4},{4,8},{8,12},{12,16},{16,20},{20,24},{24,28},{28,32},{32,36}... | collective-permute-start | bytes 1966088 | tf_op jit(solution)/shard_map/ppermute | solution.py:16
  230.4 1.5 copy-start.9
  234.5 1.2 copy-start.11
  236.1 60.8 %copy-start.1 = (bf16[1000,640]{1,0:T(8,128)(2,1)S(1)}, bf16[1000,640]{1,0:T(8,128)(2,1)}, u32[]{:S(2)}) copy-start(bf16[1000,640]{1,0:T(8,128)(2,1)} %param.8) | copy-start | bytes 3840004
Sparse Core Ops, SparseCore 0:
  54.6 84.5 reduce-scatter.1
  169.0 54.4 all-reduce.2
  239.7 55.4 all-reduce.4
where the time goes:
time: 304 us; the launch traced here: 303 us
  waiting for transfers between devices  161 us (53%)
  local copies, waits for them, and re-layouts  51.4 us (17%)
  blocking collectives  37.5 us (12%)
  matrix products  22.1 us (7%)
  other arithmetic  15.1 us (5%)
  between operations  13.5 us (4%)
  starting transfers between devices  3.32 us (1%)
    psum x2, waiting for transfers between devices, body(): lax.psum(jnp.dot(mixed, out_weight[depth], preferred_element_type=jnp.flo...  99.9 us
    reduce_scatter x1, waiting for transfers between devices, body(): lax.psum_scatter((rows * inside[:, None]).astype(jnp.bfloat16), 'seg', sc...  60.6 us
    all_gather x1, blocking collectives, body(): book_ids = lax.all_gather(token_ids, 'seg', axis=0, tiled=True)  22.9 us
    dot_general x6, local copies, waits for them, and re-layouts, project(): jnp.dot(normed, weight[depth], preferred_element_type=jnp.float32)  21.8 us
    gather x1, local copies, waits for them, and re-layouts, body(): rows = jnp.take(embed_table, clamped, axis=0).astype(jnp.float32)  17.7 us
    all_gather x1, blocking collectives, body(): states = lax.all_gather(embedded, 'head', axis=1, tiled=True)  14.5 us
    dot_general x10, matrix products, project(): jnp.dot(normed, weight[depth], preferred_element_type=jnp.float32)  9.48 us
    convert_element_type x1, other arithmetic, body(): (rows * inside[:, None]).astype(jnp.bfloat16)  7.17 us
  transfers between devices with their start and end apart: 5, of which 3 were waited for; matrix products, arithmetic and copies ran while one was open for 13% of the time, Pallas kernels for 0%

commit v1 on v0

--- a/solution.py
+++ b/solution.py
@@ -1,13 +1,21 @@
+import functools
+
 import jax
 import jax.numpy as jnp
+import numpy as np
 from jax import lax
+from jax.experimental import pallas as pl
+from jax.experimental.pallas import tpu as pltpu
 from jax.sharding import PartitionSpec as P
 
 HD = 64
 LAYERS = 2
-
-
 EPSILON = 1e-05
+SLOTS = 32
+MESH = pl.DeviceIdType.MESH
+F32 = jnp.float32
+BF16 = jnp.bfloat16
+I32 = jnp.int32
 
 
 def shifted(value, axis, steps):
@@ -49,7 +57,7 @@
     return mixed.astype(jnp.bfloat16).reshape(count, -1)
 
 
-def body(token_ids, embed_table, norm_gains, query_weight, key_weight, value_weight, out_weight):
+def general(token_ids, embed_table, norm_gains, query_weight, key_weight, value_weight, out_weight):
     seg_len = token_ids.shape[0]
     head_count = lax.axis_size("head")
     local_heads = query_weight.shape[2] // HD
@@ -98,6 +106,440 @@
     return lax.dynamic_slice_in_dim(residual, row_start, row_count, 0)
 
 
+def dot(a, b):
+    return jnp.dot(a, b, preferred_element_type=F32)
+
+
+def dot_nt(a, b):
+    return lax.dot_general(a, b, (((1,), (1,)), ((), ())), preferred_element_type=F32)
+
+
+def kernel(
+    n_seg, vr, t_len, cw, hw,
+    ids_hbm, tab_hbm, gain_hbm, wq_hbm, wk_hbm, wv_hbm, wo_hbm, rope_t_hbm, rope_s_hbm,
+    out_ref, flag_ref,
+    ids_v, gain_v, rope_t, rope_s, tab, wq, wk, wv, wo,
+    req_send, req_recv, flag_send, flag_recv, pk_send, pk_recv,
+    st, acc, kv_own, kv_past, q_own, o_part, mx_part, mixed,
+    part0, part1, frecv0, frecv1, comb0, comb1, rrecv0, rrecv1,
+    l_sem, w_sem, tab_sem, req_sem, flag_sem, pk_sem,
+    ag_s, ag_r, agf_s, agf_r, kv_s, kv_r, rs_s, rs_r,
+):
+    s = lax.axis_index("seg")
+    h = lax.axis_index("head")
+    chip, core = s // 2, lax.rem(s, 2)
+    n_chip = n_seg // 2
+    up, dn, opp = lax.rem(h + 1, 4), lax.rem(h + 3, 4), lax.rem(h + 2, 4)
+    sib = s + 1 - 2 * core
+    nxt, prv = lax.rem(s + 1, n_seg), lax.rem(s + n_seg - 1, n_seg)
+    blocks = (h, dn, up, opp)
+
+    def remote(src, dst, ss, rs, seg, head):
+        return pltpu.make_async_remote_copy(
+            src_ref=src, dst_ref=dst, send_sem=ss, recv_sem=rs,
+            device_id=(seg, head), device_id_type=MESH,
+        )
+
+    bar = pltpu.get_barrier_semaphore()
+
+    def hello(seg, head):
+        pl.semaphore_signal(bar, inc=1, device_id=(seg, head), device_id_type=MESH)
+
+    for other in (up, dn, opp):
+        hello(s, other)
+    hello(nxt, h)
+    hello(prv, h)
+
+    def hello_chip(k, c):
+        hello(2 * lax.rem(chip + k, n_chip) + core, h)
+        return c
+
+    lax.fori_loop(1, n_chip, hello_chip, 0)
+
+    loads = [
+        pltpu.make_async_copy(a, b, l_sem.at[i])
+        for i, (a, b) in enumerate(
+            [(ids_hbm, ids_v), (tab_hbm, tab.at[core]), (gain_hbm, gain_v),
+             (rope_t_hbm, rope_t), (rope_s_hbm, rope_s)]
+        )
+    ]
+    for c in loads:
+        c.start()
+    weights = {}
+    for layer in range(LAYERS):
+        for i, (a, b) in enumerate([(wk_hbm, wk), (wv_hbm, wv), (wq_hbm, wq), (wo_hbm, wo)]):
+            c = pltpu.make_async_copy(a.at[layer], b.at[layer], w_sem.at[layer, i])
+            c.start()
+            weights[layer, i] = c
+
+    loads[0].wait()
+    sub = lax.broadcasted_iota(I32, (t_len, t_len), 0)
+    lane = lax.broadcasted_iota(I32, (t_len, t_len), 1)
+    idr = jnp.broadcast_to(ids_v[...], (t_len, t_len))
+    idc = idr.T
+
+    def chip_of(ids):
+        return ((ids.astype(F32) + 0.5) * (1.0 / (2 * vr))).astype(I32)
+
+    pr, pc = chip_of(idr), chip_of(idc)
+    same = idr == idc
+    one = jnp.ones((), I32)
+    zero = jnp.zeros((), I32)
+    dup_row = jnp.sum(jnp.where(same & (sub < lane), one, zero), axis=0, keepdims=True)
+    dup_col = jnp.sum(jnp.where(same & (lane < sub), one, zero), axis=1, keepdims=True)
+    first_row, first_col = dup_row == 0, dup_col == 0
+    peer = pr == pc
+    rank_row = jnp.sum(jnp.where(peer & (idc < idr) & first_col, one, zero), axis=0, keepdims=True)
+    rank_col = jnp.sum(jnp.where(peer & (idr < idc) & first_row, one, zero), axis=1, keepdims=True)
+    full = jnp.where(jnp.max(rank_row, axis=1, keepdims=True) >= SLOTS, one, zero)
+    pcol = pc[:, 0:1]
+    wanted = jnp.broadcast_to(jnp.where(first_col, pcol * t_len + rank_col, -1), (t_len, t_len))
+    local_id = idc - 2 * vr * pc + 1
+    slot_key = pcol * SLOTS + rank_col
+    lane_row = lane[0:1]
+
+    def make_request(p, c):
+        row = jnp.sum(jnp.where(wanted == p * t_len + lane, local_id, zero), axis=0, keepdims=True) - 1
+        req_send[p] = jnp.where(lane_row == t_len - 1, full, row)
+        return c
+
+    lax.fori_loop(0, n_chip, make_request, 0)
+    req_recv[chip] = req_send[chip]
+
+    pl.semaphore_wait(bar, 3 + 2 + n_chip - 1)
+
+    def send_request(k, c):
+        p = lax.rem(chip + k, n_chip)
+        remote(req_send.at[p], req_recv.at[chip], req_sem.at[0], req_sem.at[1], 2 * p + core, h).start()
+        return c
+
+    lax.fori_loop(1, n_chip, send_request, 0)
+    tab_copy = remote(tab_hbm, tab.at[core], tab_sem.at[0], tab_sem.at[1], sib, h)
+    tab_copy.start()
+    loads[1].wait()
+    others = req_recv.at[pl.ds(0, n_chip - 1)]
+    pltpu.make_async_copy(others, others, req_sem.at[1]).wait()
+
+    reqs = jnp.concatenate([req_recv[p] for p in range(n_chip)], axis=0)
+    any_full = jnp.max(reqs, axis=0, keepdims=True)
+    any_full = jnp.max(jnp.where(lane_row == t_len - 1, any_full, zero), axis=1, keepdims=True)
+    any_full = jnp.broadcast_to(any_full, (8, t_len))
+    flag_send[...] = any_full
+    flag_copy = remote(flag_send, flag_recv, flag_sem.at[0], flag_sem.at[1], sib, h)
+    flag_copy.start()
+
+    if n_chip < t_len:
+        reqs = jnp.concatenate([reqs, jnp.zeros((t_len - n_chip, t_len), I32)], axis=0)
+    reqs_t = reqs.T
+    group = min(4, n_chip)
+    row_iota = lax.broadcasted_iota(I32, (SLOTS, vr), 1)
+    hot = [
+        jnp.concatenate(
+            [jnp.broadcast_to(reqs_t[:SLOTS, g + i:g + i + 1], (SLOTS, vr)) - row_iota for i in range(group)],
+            axis=0,
+        )
+        for g in range(0, n_chip, group)
+    ]
+    tab_copy.wait_recv()
+    for gi, g in enumerate(range(0, n_chip, group)):
+        lo = jnp.where(hot[gi] == 0, 1.0, 0.0).astype(BF16)
+        hi = jnp.where(hot[gi] == vr, 1.0, 0.0).astype(BF16)
+        rows = (dot(lo, tab[0]) + dot(hi, tab[1])).astype(BF16)
+        for i in range(group):
+            pk_send[g + i] = rows[i * SLOTS:(i + 1) * SLOTS]
+
+    pk_recv[chip] = pk_send[chip]
+
+    def send_rows(k, c):
+        p = lax.rem(chip + k, n_chip)
+        remote(pk_send.at[p], pk_recv.at[chip], pk_sem.at[0], pk_sem.at[1], 2 * p + core, h).start()
+        return c
+
+    lax.fori_loop(1, n_chip, send_rows, 0)
+
+    for c in loads[2:]:
+        c.wait()
+    cos_t, sin_t = rope_t[0], rope_t[1]
+    cos_s, sin_s = rope_s[0, pl.ds(s, 1), :], rope_s[1, pl.ds(s, 1), :]
+    cosine = cos_t * cos_s - sin_t * sin_s
+    sine = sin_t * cos_s + cos_t * sin_s
+    lane128 = lax.broadcasted_iota(I32, (t_len, 128), 1)
+    front = lax.rem(lane128, HD) < HD // 2
+    sine = jnp.where(front, -sine, sine)
+
+    def rope(x, scale):
+        pieces = []
+        for j in range(0, hw, 128):
+            y = x[:, j:j + 128] * scale
+            partner = jnp.where(front, pltpu.roll(y, 128 - HD // 2, 1), pltpu.roll(y, HD // 2, 1))
+            pieces.append(y * cosine + partner * sine)
+        return jnp.concatenate(pieces, axis=1)
+
+    slots_iota = lax.broadcasted_iota(I32, (t_len, n_chip * SLOTS), 1)
+    unpack = jnp.where(jnp.broadcast_to(slot_key, slots_iota.shape) == slots_iota, 1.0, 0.0).astype(BF16)
+
+    others = pk_recv.at[pl.ds(0, n_chip - 1)]
+    pltpu.make_async_copy(others, others, pk_sem.at[1]).wait()
+    packed = pk_recv[...].reshape(n_chip * SLOTS, cw)
+    st[0, 0] = dot(unpack, packed).astype(BF16)
+
+    causal = lane[:, :t_len] <= sub[:, :t_len]
+    causal2 = jnp.concatenate([causal, causal], axis=0)
+    head_a = lane128 < HD
+    ones = jnp.ones((t_len, 128), BF16)
+    half_t = t_len // 2
+    sends = []
+
+    for layer in range(LAYERS):
+        quarter = t_len // 4
+        ups, dns, fws = [], [], []
+        for c in range(4):
+            a = pl.ds(c * quarter, quarter)
+            e = 3 - c
+            b = pl.ds(e * quarter, quarter)
+            cu = remote(st.at[layer, 0, a], st.at[layer, 1, a], ag_s.at[layer, 0, c], ag_r.at[layer, 0, c], s, up)
+            cd = remote(st.at[layer, 0, b], st.at[layer, 2, b], ag_s.at[layer, 1, e], ag_r.at[layer, 1, e], s, dn)
+            cu.start()
+            cd.start()
+            ups.append(cu)
+            dns.append(cd)
+
+        def project(k, first):
+            x = st[layer, k].astype(F32)
+            rows = pl.ds(pl.multiple_of(blocks[k] * cw, cw), cw)
+            cols = pl.ds(pl.multiple_of(blocks[k] * cw, 128), cw)
+            gain = gain_v[pl.ds(layer, 1), cols]
+            xg = (x * gain).astype(BF16)
+            for i, w in enumerate((wk, wv, wq)):
+                y = dot(xg, w[layer, rows, :])
+                if first:
+                    acc[i] = y
+                else:
+                    acc[i] += y
+            return jnp.sum(x * x, axis=1, keepdims=True)
+
+        for i in range(3):
+            weights[layer, i].wait()
+        square = project(0, True)
+        for c in range(2):
+            a = pl.ds(c * quarter, quarter)
+            e = 3 - c
+            b = pl.ds(e * quarter, quarter)
+            ups[c].wait_recv()
+            fu = remote(st.at[layer, 1, a], st.at[layer, 3, a], agf_s.at[layer, c], agf_r.at[layer, c], s, up)
+            fu.start()
+            dns[c].wait_recv()
+            fd = remote(st.at[layer, 2, b], st.at[layer, 3, b], agf_s.at[layer, e], agf_r.at[layer, e], s, dn)
+            fd.start()
+            fws += [fu, fd]
+        for c in range(2, 4):
+            ups[c].wait_recv()
+        square += project(1, False)
+        for c in range(2, 4):
+            dns[c].wait_recv()
+        square += project(2, False)
+        for f in fws:
+            f.wait_recv()
+        square += project(3, False)
+        sends += ups + dns + fws
+        scale = lax.rsqrt(square * (1.0 / (4 * cw)) + EPSILON)
+
+        kv_own[layer, 0] = rope(acc[0], scale).astype(BF16)
+        k_copy = remote(kv_own.at[layer, 0], kv_past.at[layer, 0], kv_s.at[layer, 0], kv_r.at[layer, 0], nxt, h)
+        k_copy.start()
+        kv_own[layer, 1] = (acc[1] * scale).astype(BF16)
+        v_copy = remote(kv_own.at[layer, 1], kv_past.at[layer, 1], kv_s.at[layer, 1], kv_r.at[layer, 1], nxt, h)
+        v_copy.start()
+        sends += [k_copy, v_copy]
+        q_own[...] = (rope(acc[2], scale) * HD ** (-0.5)).astype(BF16)
+
+        def queries_of(j):
+            q = q_own[:, j:j + 128]
+            none = jnp.zeros_like(q)
+            return jnp.concatenate([jnp.where(head_a, q, none), jnp.where(head_a, none, q)], axis=0)
+
+        for i, j in enumerate(range(0, hw, 128)):
+            scores = dot_nt(queries_of(j), kv_own[layer, 0, :, j:j + 128])
+            scores = jnp.where(causal2, scores, -1e30)
+            top = jnp.max(scores, axis=1, keepdims=True)
+            e = jnp.exp(scores - top).astype(BF16)
+            values = jnp.concatenate([kv_own[layer, 1, :, j:j + 128], ones], axis=1)
+            o_part[i] = dot(e, values)
+            mx_part[i] = jnp.broadcast_to(top, (2 * t_len, 128))
+        k_copy.wait_recv()
+        v_copy.wait_recv()
+        for i, j in enumerate(range(0, hw, 128)):
+            scores = dot_nt(queries_of(j), kv_past[layer, 0, :, j:j + 128])
+            scores = jnp.where(s > 0, scores, -1e30)
+            old = mx_part[i]
+            top = jnp.maximum(old, jnp.max(scores, axis=1, keepdims=True))
+            e = jnp.exp(scores - top).astype(BF16)
+            keep = jnp.exp(old - top)
+            values = jnp.concatenate([kv_past[layer, 1, :, j:j + 128], ones], axis=1)
+            o = dot(e, values)
+            num = o_part[i, :, :128] * keep + o[:, :128]
+            den = o_part[i, :, 128:] * keep + o[:, 128:]
+            m = num / den
+            mixed[:, j:j + 128] = jnp.where(head_a, m[:t_len], m[t_len:]).astype(BF16)
+
+        weights[layer, 3].wait()
+        last = layer == LAYERS - 1
+        part, comb, frecv, rrecv = (
+            (part1, comb1, frecv1, rrecv1) if last else (part0, comb0, frecv0, rrecv0)
+        )
+        n_row = part.shape[1]
+        lo, hi = pl.ds(0, n_row // 2), pl.ds(n_row // 2, n_row // 2)
+
+        def send(i, src, dst, to):
+            c = remote(src, dst, rs_s.at[layer, i], rs_r.at[layer, i], s, to)
+            c.start()
+            sends.append(c)
+            return c
+
+        def far():
+            return [
+                send(0, part.at[opp, lo], frecv.at[0], up),
+                send(1, part.at[opp, hi], frecv.at[1], dn),
+            ]
+
+        if last:
+            for b in range(4):
+                y = dot(mixed[...], wo[layer, :, b * cw:(b + 1) * cw]).astype(BF16)
+                for d in range(4):
+                    part[d, :, b * cw:(b + 1) * cw] = y[d * n_row:(d + 1) * n_row]
+            f = far()
+        else:
+            for b in (opp, up, dn, h):
+                y = dot(mixed[...], wo[layer, :, pl.ds(pl.multiple_of(b * cw, 128), cw)])
+                part[b] = y.astype(BF16)
+                if b is opp:
+                    f = far()
+        r = [
+            send(2, part.at[up, hi], rrecv.at[0, hi], up),
+            send(3, part.at[dn, lo], rrecv.at[1, lo], dn),
+        ]
+        f[0].wait_recv()
+        comb[0] = (part[up, lo].astype(F32) + frecv[0].astype(F32)).astype(BF16)
+        r.append(send(4, comb.at[0], rrecv.at[0, lo], up))
+        f[1].wait_recv()
+        comb[1] = (part[dn, hi].astype(F32) + frecv[1].astype(F32)).astype(BF16)
+        r.append(send(5, comb.at[1], rrecv.at[1, hi], dn))
+        for c in r:
+            c.wait_recv()
+        total = part[h].astype(F32) + rrecv[0].astype(F32) + rrecv[1].astype(F32)
+        if last:
+            for k in range(4):
+                cols = pl.ds(pl.multiple_of(blocks[k] * cw, 128), cw)
+                rows = pl.ds(pl.multiple_of(h * n_row, n_row), n_row)
+                out_ref[:, cols] = st[layer, k, rows, :].astype(F32)
+            out_ref[...] += total
+        else:
+            st[layer + 1, 0] = (st[layer, 0].astype(F32) + total).astype(BF16)
+
+    flag_copy.wait()
+    flag_ref[...] = jnp.maximum(flag_send[...], flag_recv[...])
+    tab_copy.wait_send()
+    others = req_send.at[pl.ds(0, n_chip - 1)]
+    pltpu.make_async_copy(others, others, req_sem.at[0]).wait()
+    others = pk_send.at[pl.ds(0, n_chip - 1)]
+    pltpu.make_async_copy(others, others, pk_sem.at[0]).wait()
+    for c in sends:
+        c.wait_send()
+
+
+def rotary_tables(n_seg, t_len):
+    freq = 10000.0 ** (-np.arange(HD // 2, dtype=np.float64) / (HD // 2))
+    freq = np.tile(freq, 128 // (HD // 2))[None]
+    local = np.arange(t_len, dtype=np.float64)[:, None] * freq
+    start = (np.arange(n_seg, dtype=np.float64) * t_len)[:, None] * freq
+    both = lambda a: np.stack([np.cos(a), np.sin(a)]).astype(np.float32)
+    return both(local), both(start)
+
+
+def body(n_seg, token_ids, embed_table, norm_gains, query_weight, key_weight, value_weight, out_weight):
+    t_len = token_ids.shape[0]
+    vr, cw = embed_table.shape
+    hw = query_weight.shape[2]
+    n_chip = n_seg // 2
+    rope_t, rope_s = rotary_tables(n_seg, t_len)
+    rows = t_len // 4
+    vmem = pltpu.VMEM
+    dma = pltpu.SemaphoreType.DMA
+    any_spec = pl.BlockSpec(memory_space=pl.ANY)
+    vmem_spec = pl.BlockSpec(memory_space=pltpu.VMEM)
+    out, flag = pl.pallas_call(
+        functools.partial(kernel, n_seg, vr, t_len, cw, hw),
+        out_shape=(
+            jax.ShapeDtypeStruct((rows, 4 * cw), F32),
+            jax.ShapeDtypeStruct((8, t_len), I32),
+        ),
+        in_specs=[any_spec] * 9,
+        out_specs=(vmem_spec, vmem_spec),
+        scratch_shapes=[
+            vmem((1, t_len), I32),
+            vmem(norm_gains.shape, F32),
+            vmem(rope_t.shape, F32),
+            vmem(rope_s.shape, F32),
+            vmem((2, vr, cw), BF16),
+            vmem(query_weight.shape, BF16),
+            vmem(key_weight.shape, BF16),
+            vmem(value_weight.shape, BF16),
+            vmem(out_weight.shape, BF16),
+            vmem((n_chip, 1, t_len), I32),
+            vmem((n_chip, 1, t_len), I32),
+            vmem((8, t_len), I32),
+            vmem((8, t_len), I32),
+            vmem((n_chip, SLOTS, cw), BF16),
+            vmem((n_chip, SLOTS, cw), BF16),
+            vmem((LAYERS, 4, t_len, cw), BF16),
+            vmem((3, t_len, hw), F32),
+            vmem((LAYERS, 2, t_len, hw), BF16),
+            vmem((LAYERS, 2, t_len, hw), BF16),
+            vmem((t_len, hw), BF16),
+            vmem((hw // 128, 2 * t_len, 256), F32),
+            vmem((hw // 128, 2 * t_len, 128), F32),
+            vmem((t_len, hw), BF16),
+            vmem((4, t_len, cw), BF16),
+            vmem((4, rows, 4 * cw), BF16),
+            vmem((2, t_len // 2, cw), BF16),
+            vmem((2, rows // 2, 4 * cw), BF16),
+            vmem((2, t_len // 2, cw), BF16),
+            vmem((2, rows // 2, 4 * cw), BF16),
+            vmem((2, t_len, cw), BF16),
+            vmem((2, rows, 4 * cw), BF16),
+            dma((5,)),
+            dma((LAYERS, 4)),
+            dma((2,)),
+            dma((2,)),
+            dma((2,)),
+            dma((2,)),
+            dma((LAYERS, 2, 4)),
+            dma((LAYERS, 2, 4)),
+            dma((LAYERS, 4)),
+            dma((LAYERS, 4)),
+            dma((LAYERS, 2)),
+            dma((LAYERS, 2)),
+            dma((LAYERS, 6)),
+            dma((LAYERS, 6)),
+        ],
+        compiler_params=pltpu.CompilerParams(
+            collective_id=0, has_side_effects=True, vmem_limit_bytes=56 * 2 ** 20
+        ),
+        name="decoder",
+    )(
+        token_ids.reshape(1, t_len), embed_table, norm_gains,
+        query_weight, key_weight, value_weight, out_weight,
+        jnp.asarray(rope_t), jnp.asarray(rope_s),
+    )
+    return lax.cond(
+        flag[0, 0] > 0,
+        lambda: general(
+            token_ids, embed_table, norm_gains, query_weight, key_weight, value_weight, out_weight
+        ),
+        lambda: out.astype(BF16),
+    )
+
+
 def solution(mesh):
     placed = (
         P("seg"),
@@ -109,5 +551,6 @@
         P(None, "head", None),
     )
     return jax.shard_map(
-        body, mesh=mesh, in_specs=placed, out_specs=P(("seg", "head"), None), check_vma=False
+        functools.partial(body, mesh.shape["seg"]),
+        mesh=mesh, in_specs=placed, out_specs=P(("seg", "head"), None), check_vma=False,
     )

time: 304 us -> 88 us (0.29)
  waiting for transfers between devices: 161 us -> 0 us
  Pallas kernels: 0 us -> 71.9 us
  local copies, waits for them, and re-layouts: 51.4 us -> 1.2 us
  blocking collectives: 37.5 us -> 0 us
  matrix products: 22.1 us -> 0 us
  other arithmetic: 15.1 us -> 0.68 us
  starting transfers between devices: 3.32 us -> 0 us
    psum x2 -> x0, waiting for transfers between devices: 99.9 us -> none  [body(): lax.psum(jnp.dot(mixed, out_weight[depth], preferred_element_type=jnp.flo...]
    pallas_call x0 -> x1, Pallas kernels: none -> 71.9 us  [body(): pl.pallas_call(functools.partial(kernel, n_seg, vr, t_len, cw, hw), out_s...]
    reduce_scatter x1 -> x0, waiting for transfers between devices: 60.6 us -> none  [body(): lax.psum_scatter((rows * inside[:, None]).astype(jnp.bfloat16), 'seg', sc...]
    all_gather x2 -> x0, blocking collectives: 37.5 us -> none  [the longest x1 22.9 us: body(): book_ids = lax.all_gather(token_ids, 'seg', axis=0, tiled=True)]
    dot_general x6 -> x0, local copies, waits for them, and re-layouts: 21.8 us -> none  [project(): jnp.dot(normed, weight[depth], preferred_element_type=jnp.float32)]
    gather x1 -> x0, local copies, waits for them, and re-layouts: 17.7 us -> none  [body(): rows = jnp.take(embed_table, clamped, axis=0).astype(jnp.float32)]
    dot_general x14 -> x0, matrix products: 17.2 us -> none  [the longest x10 9.48 us: project(): jnp.dot(normed, weight[depth], preferred_element_type=jnp.float32)]
    convert_element_type x6 -> x1, other arithmetic: 9.38 us -> 0.68 us  [body(): out.astype(BF16)]
  transfers between devices with their start and end apart: 5 -> 0, of which waited for: 3 -> 0; matrix products, arithmetic and copies ran while one was open for 13% -> 0% of each run, Pallas kernels for 0% -> 0%
where the time goes in v1:
time: 88 us; the launch traced here: 87.8 us
  Pallas kernels  71.9 us (82%)
  between operations  14.1 us (16%)
  local copies, waits for them, and re-layouts  1.2 us (1%)
    pallas_call x1, Pallas kernels, body(): pl.pallas_call(functools.partial(kernel, n_seg, vr, t_len, cw, hw), out_s...  71.9 us

profile of v1, /device:TPU:0, one launch (start us, length us, event | category | flops | bytes accessed | tf_op | source)
XLA Modules:
  0.0 87.8 jit_solution(8318441979548571178)
XLA Ops:
  6.5 0.0 copy-start
  6.5 0.0 copy-start.8
  6.5 0.0 copy-start.10
  6.5 71.9 %decoder.1 = (f32[32,2560]{1,0:T(8,128)S(1)}, s32[8,128]{1,0:T(8,128)}) custom-call(s32[1,128]{1,0:T(1,128)} %bitcast.102, bf16[1000,640]{1,0:T(8,128)(2,1)} %tab_hbm.1, f32[2,2560]{1,0:T(2,128)} %gain_hbm.1, bf16[2,2560,512]{2,1,0:T(8,128)(2,1)} %wq_hbm.1, bf16[2,2560,512]{2,1,0:T(8,128)(2,1)} %wk_hbm.1, bf16[2,2560,512]{2,1,0:T(8,128)(2,1)} %wv_hbm.1, ...), custom_call_target="tpu_custom_call" | custom-call | tf_op jit(solution)/shard_map/decoder/pallas_call | solution.py:470
  78.4 1.2 %slice.73 = s32[1,1]{1,0:T(1,128)} slice(s32[8,128]{1,0:T(8,128)} %get-tuple-element.32), slice={[0:1], [0:1]} | slice | bytes 8 | tf_op jit(solution)/shard_map/slice | solution.py:535
  80.3 0.0 copy-done
  80.3 0.0 copy-done.8
  80.3 0.0 copy-done.10
  80.3 0.7 conditional.1
  80.3 0.7 convert_element_type.68
Async XLA Ops:
  6.5 73.7 %copy-start = (bf16[1000,640]{1,0:T(8,128)(2,1)S(1)}, bf16[1000,640]{1,0:T(8,128)(2,1)}, u32[]{:S(2)}) copy-start(bf16[1000,640]{1,0:T(8,128)(2,1)} %tab_hbm.1) | copy-start | bytes 3840004
  6.5 73.7 %copy-start.8 = (f32[2,2560]{1,0:T(2,128)S(1)}, f32[2,2560]{1,0:T(2,128)}, u32[]{:S(2)}) copy-start(f32[2,2560]{1,0:T(2,128)} %gain_hbm.1) | copy-start | bytes 61444
  6.5 73.8 %copy-start.10 = (s32[128]{0:T(128)S(1)}, s32[128]{0:T(128)}, u32[]{:S(2)}) copy-start(s32[128]{0:T(128)} %param.11) | copy-start | bytes 1540

commit v2 on v1

--- a/solution.py
+++ b/solution.py
@@ -11,101 +11,13 @@
 HD = 64
 LAYERS = 2
 EPSILON = 1e-05
-SLOTS = 32
+SLOTS, ALL_SLOTS = 32, 128
 MESH = pl.DeviceIdType.MESH
 F32 = jnp.float32
 BF16 = jnp.bfloat16
 I32 = jnp.int32
 
 
-def shifted(value, axis, steps):
-    count = lax.axis_size(axis)
-    leading, last = (max(0, -steps), min(count, count - steps))
-    return lax.ppermute(value, axis, [(source, source + steps) for source in range(leading, last)])
-
-
-def rotate(field, positions):
-    half_dim = field.shape[-1] // 2
-    frequency = 10000.0 ** (-jnp.arange(half_dim, dtype=jnp.float32) / half_dim)
-    angles = positions.astype(jnp.float32)[:, None] * frequency[None, :]
-    cosine = jnp.cos(angles)[:, None, :]
-    sine = jnp.sin(angles)[:, None, :]
-    front = field[..., :half_dim]
-    back = field[..., half_dim:]
-    return jnp.concatenate([front * cosine - back * sine, front * sine + back * cosine], axis=-1)
-
-
-def normalize(states, gain):
-    widened = states.astype(jnp.float32)
-    mean_square = jnp.mean(widened * widened, axis=-1, keepdims=True)
-    return (widened * lax.rsqrt(mean_square + EPSILON) * gain).astype(jnp.bfloat16)
-
-
-def attend_block(queries, keys_all, values_all, has_memory):
-    count = queries.shape[0]
-    scores = jnp.einsum(
-        "qhd,khd->hqk", queries, keys_all, preferred_element_type=jnp.float32
-    ) * queries.shape[-1] ** (-0.5)
-    query_place = jnp.arange(count, dtype=jnp.int32)[:, None]
-    key_place = jnp.arange(2 * count, dtype=jnp.int32)[None, :]
-    allowed = jnp.where(key_place < count, has_memory, key_place - count <= query_place)
-    scores = jnp.where(allowed[None], scores, -1e30)
-    top_score = jnp.max(scores, axis=-1, keepdims=True)
-    weights = jnp.exp(scores - top_score)
-    probs = (weights / jnp.sum(weights, axis=-1, keepdims=True)).astype(jnp.bfloat16)
-    mixed = jnp.einsum("hqk,khd->qhd", probs, values_all, preferred_element_type=jnp.float32)
-    return mixed.astype(jnp.bfloat16).reshape(count, -1)
-
-
-def general(token_ids, embed_table, norm_gains, query_weight, key_weight, value_weight, out_weight):
-    seg_len = token_ids.shape[0]
-    head_count = lax.axis_size("head")
-    local_heads = query_weight.shape[2] // HD
-    book_ids = lax.all_gather(token_ids, "seg", axis=0, tiled=True)
-    vocab_rows = embed_table.shape[0]
-    seg_index = lax.axis_index("seg")
-    vocab_start = seg_index * vocab_rows
-    chosen = book_ids - vocab_start
-    inside = ((chosen >= 0) & (chosen < vocab_rows)).astype(jnp.float32)
-    clamped = jnp.clip(chosen, 0, vocab_rows - 1)
-    rows = jnp.take(embed_table, clamped, axis=0).astype(jnp.float32)
-    embedded = lax.psum_scatter(
-        (rows * inside[:, None]).astype(jnp.bfloat16), "seg", scatter_dimension=0, tiled=True
-    )
-    states = lax.all_gather(embedded, "head", axis=1, tiled=True)
-    positions = seg_index * seg_len + jnp.arange(seg_len, dtype=jnp.int32)
-    has_memory = seg_index > 0
-    row_count = seg_len // head_count
-    row_start = lax.axis_index("head") * row_count
-
-    def project(normed, weight, depth):
-        return jnp.dot(normed, weight[depth], preferred_element_type=jnp.float32).reshape(
-            seg_len, local_heads, HD
-        )
-
-    normed = normalize(states, norm_gains[0])
-    residual = states
-    for depth in range(LAYERS):
-        queries = rotate(project(normed, query_weight, depth), positions).astype(jnp.bfloat16)
-        keys_now = rotate(project(normed, key_weight, depth), positions).astype(jnp.bfloat16)
-        values_now = project(normed, value_weight, depth).astype(jnp.bfloat16)
-        normed_past = shifted(normed, "seg", 1)
-        keys_past = rotate(project(normed_past, key_weight, depth), positions - seg_len).astype(
-            jnp.bfloat16
-        )
-        values_past = project(normed_past, value_weight, depth).astype(jnp.bfloat16)
-        keys_all = jnp.concatenate([keys_past, keys_now], 0)
-        values_all = jnp.concatenate([values_past, values_now], 0)
-        mixed = attend_block(queries, keys_all, values_all, has_memory)
-        summed = lax.psum(
-            jnp.dot(mixed, out_weight[depth], preferred_element_type=jnp.float32), "head"
-        )
-        residual = (residual.astype(jnp.float32) + summed).astype(jnp.bfloat16)
-        if depth + 1 < LAYERS:
-            normed = normalize(residual, norm_gains[depth + 1])
-    return lax.dynamic_slice_in_dim(residual, row_start, row_count, 0)
-
-
 def dot(a, b):
     return jnp.dot(a, b, preferred_element_type=F32)
 
@@ -115,7 +27,7 @@
 
 
 def kernel(
-    n_seg, vr, t_len, cw, hw,
+    slots, n_seg, vr, t_len, cw, hw,
     ids_hbm, tab_hbm, gain_hbm, wq_hbm, wk_hbm, wv_hbm, wo_hbm, rope_t_hbm, rope_s_hbm,
     out_ref, flag_ref,
     ids_v, gain_v, rope_t, rope_s, tab, wq, wk, wv, wo,
@@ -145,9 +57,9 @@
     def hello(seg, head):
         pl.semaphore_signal(bar, inc=1, device_id=(seg, head), device_id_type=MESH)
 
-    for other in (up, dn, opp):
+    for other in (up, dn):
         hello(s, other)
-    hello(nxt, h)
+    hello(sib, h)
     hello(prv, h)
 
     def hello_chip(k, c):
@@ -191,22 +103,22 @@
     peer = pr == pc
     rank_row = jnp.sum(jnp.where(peer & (idc < idr) & first_col, one, zero), axis=0, keepdims=True)
     rank_col = jnp.sum(jnp.where(peer & (idr < idc) & first_row, one, zero), axis=1, keepdims=True)
-    full = jnp.where(jnp.max(rank_row, axis=1, keepdims=True) >= SLOTS, one, zero)
+    full = jnp.where(jnp.max(rank_row, axis=1, keepdims=True) >= slots, one, zero)
     pcol = pc[:, 0:1]
     wanted = jnp.broadcast_to(jnp.where(first_col, pcol * t_len + rank_col, -1), (t_len, t_len))
     local_id = idc - 2 * vr * pc + 1
-    slot_key = pcol * SLOTS + rank_col
+    slot_key = pcol * slots + rank_col
     lane_row = lane[0:1]
 
     def make_request(p, c):
         row = jnp.sum(jnp.where(wanted == p * t_len + lane, local_id, zero), axis=0, keepdims=True) - 1
-        req_send[p] = jnp.where(lane_row == t_len - 1, full, row)
+        req_send[p] = jnp.where(lane_row == t_len - 1, full, row) if slots < t_len else row
         return c
 
     lax.fori_loop(0, n_chip, make_request, 0)
     req_recv[chip] = req_send[chip]
 
-    pl.semaphore_wait(bar, 3 + 2 + n_chip - 1)
+    pl.semaphore_wait(bar, 2 + 2 + n_chip - 1)
 
     def send_request(k, c):
         p = lax.rem(chip + k, n_chip)
@@ -223,19 +135,18 @@
     reqs = jnp.concatenate([req_recv[p] for p in range(n_chip)], axis=0)
     any_full = jnp.max(reqs, axis=0, keepdims=True)
     any_full = jnp.max(jnp.where(lane_row == t_len - 1, any_full, zero), axis=1, keepdims=True)
-    any_full = jnp.broadcast_to(any_full, (8, t_len))
-    flag_send[...] = any_full
+    flag_send[...] = jnp.broadcast_to(any_full, (8, t_len))
     flag_copy = remote(flag_send, flag_recv, flag_sem.at[0], flag_sem.at[1], sib, h)
     flag_copy.start()
 
     if n_chip < t_len:
         reqs = jnp.concatenate([reqs, jnp.zeros((t_len - n_chip, t_len), I32)], axis=0)
     reqs_t = reqs.T
-    group = min(4, n_chip)
-    row_iota = lax.broadcasted_iota(I32, (SLOTS, vr), 1)
+    group = min(t_len // slots, n_chip)
+    row_iota = lax.broadcasted_iota(I32, (slots, vr), 1)
     hot = [
         jnp.concatenate(
-            [jnp.broadcast_to(reqs_t[:SLOTS, g + i:g + i + 1], (SLOTS, vr)) - row_iota for i in range(group)],
+            [jnp.broadcast_to(reqs_t[:slots, g + i:g + i + 1], (slots, vr)) - row_iota for i in range(group)],
             axis=0,
         )
         for g in range(0, n_chip, group)
@@ -246,7 +157,7 @@
         hi = jnp.where(hot[gi] == vr, 1.0, 0.0).astype(BF16)
         rows = (dot(lo, tab[0]) + dot(hi, tab[1])).astype(BF16)
         for i in range(group):
-            pk_send[g + i] = rows[i * SLOTS:(i + 1) * SLOTS]
+            pk_send[g + i] = rows[i * slots:(i + 1) * slots]
 
     pk_recv[chip] = pk_send[chip]
 
@@ -275,12 +186,12 @@
             pieces.append(y * cosine + partner * sine)
         return jnp.concatenate(pieces, axis=1)
 
-    slots_iota = lax.broadcasted_iota(I32, (t_len, n_chip * SLOTS), 1)
+    slots_iota = lax.broadcasted_iota(I32, (t_len, n_chip * slots), 1)
     unpack = jnp.where(jnp.broadcast_to(slot_key, slots_iota.shape) == slots_iota, 1.0, 0.0).astype(BF16)
 
     others = pk_recv.at[pl.ds(0, n_chip - 1)]
     pltpu.make_async_copy(others, others, pk_sem.at[1]).wait()
-    packed = pk_recv[...].reshape(n_chip * SLOTS, cw)
+    packed = pk_recv[...].reshape(n_chip * slots, cw)
     st[0, 0] = dot(unpack, packed).astype(BF16)
 
     causal = lane[:, :t_len] <= sub[:, :t_len]
@@ -437,7 +348,7 @@
             st[layer + 1, 0] = (st[layer, 0].astype(F32) + total).astype(BF16)
 
     flag_copy.wait()
-    flag_ref[...] = jnp.maximum(flag_send[...], flag_recv[...])
+    flag_ref[0, 0] = jnp.max(jnp.maximum(flag_send[...], flag_recv[...]))
     tab_copy.wait_send()
     others = req_send.at[pl.ds(0, n_chip - 1)]
     pltpu.make_async_copy(others, others, req_sem.at[0]).wait()
@@ -456,7 +367,7 @@
     return both(local), both(start)
 
 
-def body(n_seg, token_ids, embed_table, norm_gains, query_weight, key_weight, value_weight, out_weight):
+def run(slots, n_seg, token_ids, embed_table, norm_gains, query_weight, key_weight, value_weight, out_weight):
     t_len = token_ids.shape[0]
     vr, cw = embed_table.shape
     hw = query_weight.shape[2]
@@ -467,14 +378,14 @@
     dma = pltpu.SemaphoreType.DMA
     any_spec = pl.BlockSpec(memory_space=pl.ANY)
     vmem_spec = pl.BlockSpec(memory_space=pltpu.VMEM)
-    out, flag = pl.pallas_call(
-        functools.partial(kernel, n_seg, vr, t_len, cw, hw),
+    return pl.pallas_call(
+        functools.partial(kernel, slots, n_seg, vr, t_len, cw, hw),
         out_shape=(
             jax.ShapeDtypeStruct((rows, 4 * cw), F32),
-            jax.ShapeDtypeStruct((8, t_len), I32),
+            jax.ShapeDtypeStruct((1, 1), I32),
         ),
         in_specs=[any_spec] * 9,
-        out_specs=(vmem_spec, vmem_spec),
+        out_specs=(vmem_spec, pl.BlockSpec(memory_space=pltpu.SMEM)),
         scratch_shapes=[
             vmem((1, t_len), I32),
             vmem(norm_gains.shape, F32),
@@ -489,8 +400,8 @@
             vmem((n_chip, 1, t_len), I32),
             vmem((8, t_len), I32),
             vmem((8, t_len), I32),
-            vmem((n_chip, SLOTS, cw), BF16),
-            vmem((n_chip, SLOTS, cw), BF16),
+            vmem((n_chip, slots, cw), BF16),
+            vmem((n_chip, slots, cw), BF16),
             vmem((LAYERS, 4, t_len, cw), BF16),
             vmem((3, t_len, hw), F32),
             vmem((LAYERS, 2, t_len, hw), BF16),
@@ -523,7 +434,7 @@
             dma((LAYERS, 6)),
         ],
         compiler_params=pltpu.CompilerParams(
-            collective_id=0, has_side_effects=True, vmem_limit_bytes=56 * 2 ** 20
+            collective_id=int(slots == ALL_SLOTS), has_side_effects=True, vmem_limit_bytes=56 * 2 ** 20
         ),
         name="decoder",
     )(
@@ -531,11 +442,13 @@
         query_weight, key_weight, value_weight, out_weight,
         jnp.asarray(rope_t), jnp.asarray(rope_s),
     )
+
+
+def body(n_seg, *arrays):
+    out, flag = run(SLOTS, n_seg, *arrays)
     return lax.cond(
         flag[0, 0] > 0,
-        lambda: general(
-            token_ids, embed_table, norm_gains, query_weight, key_weight, value_weight, out_weight
-        ),
+        lambda: run(ALL_SLOTS, n_seg, *arrays)[0].astype(BF16),
         lambda: out.astype(BF16),
     )
 

time: 88 us -> 72.1 us (0.82)
  between operations: 14.1 us -> 0.7 us
  Pallas kernels: 71.9 us -> 70 us
  local copies, waits for them, and re-layouts: 1.2 us -> 0.02 us
    pallas_call x1, Pallas kernels: 71.9 us -> 70 us  [run(): pl.pallas_call(functools.partial(kernel, slots, n_seg, vr, t_len, cw, hw)...]
    slice x1 -> x0, local copies, waits for them, and re-layouts: 1.19 us -> none  [body(): flag[0, 0] > 0]
where the time goes in v2:
time: 72.1 us; the launch traced here: 71.6 us
  Pallas kernels  70 us (97%)
    pallas_call x1, Pallas kernels, run(): pl.pallas_call(functools.partial(kernel, slots, n_seg, vr, t_len, cw, hw)...  70 us

profile of v2, /device:TPU:0, one launch (start us, length us, event | category | flops | bytes accessed | tf_op | source)
XLA Modules:
  0.0 71.6 jit_solution(13531350977422268490)
XLA Ops:
  0.0 0.0 copy-start
  0.0 0.0 copy-start.1
  0.0 0.0 copy-start.2
  0.0 0.0 copy-start.3
  0.0 0.0 copy-start.4
  0.0 0.0 copy-start.5
  0.0 70.0 %decoder.3 = (f32[32,2560]{1,0:T(8,128)S(1)}, s32[1,1]{1,0:T(1,128)}) custom-call(s32[1,128]{1,0:T(1,128)} %bitcast.3, bf16[1000,640]{1,0:T(8,128)(2,1)} %tab_hbm.1, f32[2,2560]{1,0:T(2,128)} %gain_hbm.1, bf16[2,2560,512]{2,1,0:T(8,128)(2,1)} %wq_hbm.1, bf16[2,2560,512]{2,1,0:T(8,128)(2,1)} %wk_hbm.1, bf16[2,2560,512]{2,1,0:T(8,128)(2,1)} %wv_hbm.1, ...), custom_call_target="tpu_custom_call" | custom-call | tf_op jit(solution)/shard_map/decoder/pallas_call | solution.py:381
  70.7 0.0 copy-done
  70.7 0.0 copy-done.1
  70.7 0.0 copy-done.2
  70.7 0.0 copy-done.3
  70.7 0.0 copy-done.4
  70.7 0.0 copy-done.5
  70.7 0.2 conditional.6
  71.0 0.7 convert_element_type.21
Async XLA Ops:
  0.0 70.7 %copy-start = (bf16[2,2560,512]{2,1,0:T(8,128)(2,1)S(1)}, bf16[2,2560,512]{2,1,0:T(8,128)(2,1)}, u32[]{:S(2)}) copy-start(bf16[2,2560,512]{2,1,0:T(8,128)(2,1)} %wq_hbm.1) | copy-start | bytes 15728644
  0.0 70.7 %copy-start.1 = (bf16[1000,640]{1,0:T(8,128)(2,1)S(1)}, bf16[1000,640]{1,0:T(8,128)(2,1)}, u32[]{:S(2)}) copy-start(bf16[1000,640]{1,0:T(8,128)(2,1)} %tab_hbm.1) | copy-start | bytes 3840004
  0.0 70.7 %copy-start.2 = (f32[2,128,128]{2,1,0:T(8,128)S(1)}, f32[2,128,128]{2,1,0:T(8,128)}, u32[]{:S(2)}) copy-start(f32[2,128,128]{2,1,0:T(8,128)} %constant.7.clone.rope_t_hbm) | copy-start | bytes 393220
  0.0 70.7 %copy-start.3 = (f32[2,32,128]{2,1,0:T(8,128)S(1)}, f32[2,32,128]{2,1,0:T(8,128)}, u32[]{:S(2)}) copy-start(f32[2,32,128]{2,1,0:T(8,128)} %constant.8.clone.rope_s_hbm) | copy-start | bytes 98308
  0.0 70.7 %copy-start.4 = (f32[2,2560]{1,0:T(2,128)S(1)}, f32[2,2560]{1,0:T(2,128)}, u32[]{:S(2)}) copy-start(f32[2,2560]{1,0:T(2,128)} %gain_hbm.1) | copy-start | bytes 61444
  0.0 70.7 %copy-start.5 = (s32[128]{0:T(128)S(1)}, s32[128]{0:T(128)}, u32[]{:S(2)}) copy-start(s32[128]{0:T(128)} %param.13) | copy-start | bytes 1540

commit v3 on v2

v3 whole, which is shorter than its diff:
```python
import functools

import jax
import jax.numpy as jnp
import numpy as np
from jax import lax
from jax.experimental import pallas as pl
from jax.experimental.pallas import tpu as pltpu
from jax.sharding import PartitionSpec as P

HD = 64
LAYERS = 2
EPSILON = 1e-05
SLOTS, ALL_SLOTS = 24, 128
MESH = pl.DeviceIdType.MESH
F32 = jnp.float32
BF16 = jnp.bfloat16
I32 = jnp.int32


def dot(a, b):
    return jnp.dot(a, b, preferred_element_type=F32)


def dot_nt(a, b):
    return lax.dot_general(a, b, (((1,), (1,)), ((), ())), preferred_element_type=F32)


def plane(n_chip):
    nx, nz = (4, n_chip // 4) if n_chip % 4 == 0 else (1, n_chip)
    far = lambda d, n: min(d, n - d)
    slots = [
        (dx * nz + dz, dx, dz, (-dx) % nx * nz + (-dz) % nz) for dx in range(nx) for dz in range(nz)
    ]
    return nx, nz, sorted(slots, key=lambda o: far(o[1], nx) + far(o[2], nz))


def kernel(
    slots, n_seg, vr, t_len, cw, hw, f_cuts,
    ids_hbm, tab_hbm, gain_hbm, wq_hbm, wk_hbm, wv_hbm, wo_hbm, rope_t_hbm, rope_s_hbm,
    out_ref, flag_ref,
    ids_v, gain_v, rope_t, rope_s, tab, wq, wk, wv, wo,
    req_send, req_recv, flag_send, flag_recv, hot, pk_send, pk_recv,
    st, acc, kv_own, kv_past, q_own, o_part, mx_part, mixed,
    part0, part1, frecv0, frecv1, comb0, comb1, rrecv0, rrecv1,
    l_sem, w_sem, tab_sem, req_s, req_r, flag_sem, pk_s, pk_r,
    ag_s, ag_r, agf_s, agf_r, kv_s, kv_r, rs_s, rs_r,
):
    s = lax.axis_index("seg")
    h = lax.axis_index("head")
    chip, core = s // 2, lax.rem(s, 2)
    n_chip = n_seg // 2
    nx, nz, offsets = plane(n_chip)
    x, z = chip // nz, lax.rem(chip, nz)
    up, dn, opp = lax.rem(h + 1, 4), lax.rem(h + 3, 4), lax.rem(h + 2, 4)
    sib = s + 1 - 2 * core
    nxt, prv = lax.rem(s + 1, n_seg), lax.rem(s + n_seg - 1, n_seg)
    blocks = (h, dn, up, opp)

    def chip_at(dx, dz):
        return lax.rem(x + dx, nx) * nz + lax.rem(z + dz, nz)

    def remote(src, dst, ss, rs, seg, head):
        return pltpu.make_async_remote_copy(
            src_ref=src, dst_ref=dst, send_sem=ss, recv_sem=rs,
            device_id=(seg, head), device_id_type=MESH,
        )

    bar = pltpu.get_barrier_semaphore()

    def hello(seg, head):
        pl.semaphore_signal(bar, inc=1, device_id=(seg, head), device_id_type=MESH)

    for _, dx, dz, _ in offsets[:0:-1]:
        hello(2 * chip_at(dx, dz) + core, h)
    for other in (up, dn):
        hello(s, other)
    hello(sib, h)
    hello(prv, h)

    loads = [
        pltpu.make_async_copy(a, b, l_sem.at[i])
        for i, (a, b) in enumerate(
            [(ids_hbm, ids_v), (tab_hbm, tab.at[core]), (gain_hbm, gain_v),
             (rope_t_hbm, rope_t), (rope_s_hbm, rope_s)]
        )
    ]
    for c in loads:
        c.start()
    weights = {}
    for layer in range(LAYERS):
        for i, (a, b) in enumerate([(wk_hbm, wk), (wv_hbm, wv), (wq_hbm, wq), (wo_hbm, wo)]):
            c = pltpu.make_async_copy(a.at[layer], b.at[layer], w_sem.at[layer, i])
            c.start()
            weights[layer, i] = c

    loads[0].wait()
    sub = lax.broadcasted_iota(I32, (t_len, t_len), 0)
    lane = lax.broadcasted_iota(I32, (t_len, t_len), 1)
    idr = jnp.broadcast_to(ids_v[...], (t_len, t_len))
    idc = idr.T

    def chip_of(ids):
        return ((ids.astype(F32) + 0.5) * (1.0 / (2 * vr))).astype(I32)

    pr, pc = chip_of(idr), chip_of(idc)
    same = idr == idc
    one = jnp.ones((), I32)
    zero = jnp.zeros((), I32)
    dup_row = jnp.sum(jnp.where(same & (sub < lane), one, zero), axis=0, keepdims=True)
    dup_col = jnp.sum(jnp.where(same & (lane < sub), one, zero), axis=1, keepdims=True)
    first_row, first_col = dup_row == 0, dup_col == 0
    peer = pr == pc
    rank_row = jnp.sum(jnp.where(peer & (idc < idr) & first_col, one, zero), axis=0, keepdims=True)
    rank_col = jnp.sum(jnp.where(peer & (idr < idc) & first_row, one, zero), axis=1, keepdims=True)
    full = jnp.where(jnp.max(rank_row, axis=1, keepdims=True) >= slots, one, zero)
    wanted = jnp.where(first_col, pc[:, 0:1] * t_len + rank_col, -1)
    wanted = jnp.broadcast_to(wanted, (t_len, t_len)) - lane
    local_id = idc - 2 * vr * pc + 1
    lane_row = lane[0:1]
    for slot, dx, dz, _ in offsets:
        row = jnp.where(wanted == chip_at(dx, dz) * t_len, local_id, zero)
        row = jnp.sum(row, axis=0, keepdims=True) - 1
        req_send[slot] = jnp.where(lane_row == t_len - 1, full, row) if slots < t_len else row
    req_recv[0] = req_send[0]

    px = sum(jnp.where(pc >= i * nz, one, zero) for i in range(1, nx)) if nx > 1 else jnp.zeros_like(pc)
    rx, rz = px - x, pc - px * nz - z
    rel = jnp.where(rx < 0, rx + nx, rx) * nz + jnp.where(rz < 0, rz + nz, rz)
    slot_key = rel[:, 0:1] * slots + rank_col
    slots_iota = lax.broadcasted_iota(I32, (t_len, n_chip * slots), 1)
    unpack = jnp.where(jnp.broadcast_to(slot_key, slots_iota.shape) == slots_iota, 1.0, 0.0).astype(BF16)

    @pl.when(s == 0)
    def _():
        kv_past[...] = jnp.zeros_like(kv_past)

    pl.semaphore_wait(bar, 2 + 2 + n_chip - 1)

    group = min(4, n_chip)
    group_of = {o[0]: i // group for i, o in enumerate(offsets)}
    for slot, dx, dz, back in offsets[:0:-1]:
        remote(
            req_send.at[slot], req_recv.at[back], req_s.at[0], req_r.at[group_of[back]],
            2 * chip_at(dx, dz) + core, h,
        ).start()
    tab_copy = remote(tab_hbm, tab.at[core], tab_sem.at[0], tab_sem.at[1], sib, h)
    tab_copy.start()
    loads[1].wait()
    row_iota = lax.broadcasted_iota(I32, (slots, vr), 1)

    pk_copies = {}
    for f, (f0, f1) in enumerate(f_cuts):
        cols = pl.ds(f0, f1 - f0)
        for g in range(n_chip // group):
            members = offsets[g * group:(g + 1) * group]
            rows = pl.ds(g * group * slots, group * slots)
            if f == 0:
                came = req_recv.at[pl.ds(0, sum(o[0] != 0 for o in members))]
                pltpu.make_async_copy(came, came, req_r.at[g]).wait()
                asked = jnp.concatenate(
                    [req_recv[o[0]] for o in members] + [jnp.zeros((t_len - group, t_len), I32)], axis=0
                ).T
                away = jnp.concatenate(
                    [jnp.broadcast_to(asked[:slots, i:i + 1], (slots, vr)) - row_iota for i in range(group)], axis=0
                )
                if g == 0:
                    tab_copy.wait_recv()
                hot[0, rows] = jnp.where(away == 0, 1.0, 0.0).astype(BF16)
                hot[1, rows] = jnp.where(away == vr, 1.0, 0.0).astype(BF16)
            found = dot(hot[0, rows], tab[0, :, cols]) + dot(hot[1, rows], tab[1, :, cols])
            for i, (slot, dx, dz, back) in enumerate(members):
                piece = found[i * slots:(i + 1) * slots].astype(BF16)
                if slot == 0:
                    pk_recv[0, :, cols] = piece
                else:
                    pk_send[slot, :, cols] = piece
                    remote(
                        pk_send.at[slot, :, cols], pk_recv.at[back, :, cols], pk_s.at[f], pk_r.at[f],
                        2 * chip_at(dx, dz) + core, h,
                    ).start()

    reqs = jnp.concatenate([req_recv[p] for p in range(n_chip)], axis=0)
    any_full = jnp.max(reqs, axis=0, keepdims=True)
    any_full = jnp.max(jnp.where(lane_row == t_len - 1, any_full, zero), axis=1, keepdims=True)
    flag_send[...] = jnp.broadcast_to(any_full, (8, t_len))
    flag_copy = remote(flag_send, flag_recv, flag_sem.at[0], flag_sem.at[1], sib, h)
    flag_copy.start()

    for c in loads[2:]:
        c.wait()
    cos_t, sin_t = rope_t[0], rope_t[1]
    cos_s, sin_s = rope_s[0, pl.ds(s, 1), :], rope_s[1, pl.ds(s, 1), :]
    cosine = cos_t * cos_s - sin_t * sin_s
    sine = sin_t * cos_s + cos_t * sin_s
    lane128 = lax.broadcasted_iota(I32, (t_len, 128), 1)
    front = lax.rem(lane128, HD) < HD // 2
    sine = jnp.where(front, -sine, sine)

    def rope(x, scale):
        pieces = []
        for j in range(0, hw, 128):
            y = x[:, j:j + 128] * scale
            partner = jnp.where(front, pltpu.roll(y, 128 - HD // 2, 1), pltpu.roll(y, HD // 2, 1))
            pieces.append(y * cosine + partner * sine)
        return jnp.concatenate(pieces, axis=1)

    causal = lane[:, :t_len] <= sub[:, :t_len]
    causal2 = jnp.concatenate([causal, causal], axis=0)
    head_a = lane128 < HD
    ones = jnp.ones((t_len, 128), BF16)
    sends = []

    def halves(region):
        r0, r1, c0, c1 = region
        mid, cols = (r0 + r1) // 2, pl.ds(c0, c1 - c0)
        return (pl.ds(r0, mid - r0), cols), (pl.ds(mid, r1 - mid), cols)

    def share(layer, i, region):
        a, b = halves(region)
        own, low, high = st.at[layer, 0], st.at[layer, 1], st.at[layer, 2]

        def both(k, part):
            cu = remote(own.at[part], low.at[part], ag_s.at[layer, i, 0, k], ag_r.at[layer, i, 0, k], s, up)
            cd = remote(own.at[part], high.at[part], ag_s.at[layer, i, 1, k], ag_r.at[layer, i, 1, k], s, dn)
            return cu, cd

        (ua, da), (ub, db) = both(0, a), both(1, b)
        for c in (ua, db, ub, da):
            c.start()
        sends.extend([ua, db, ub, da])
        return ua, da, ub, db

    def pass_on(layer, i, region, copies):
        ua, da, ub, db = copies
        a, b = halves(region)
        low, high, far = st.at[layer, 1], st.at[layer, 2], st.at[layer, 3]
        fu = remote(low.at[a], far.at[a], agf_s.at[layer, i, 0], agf_r.at[layer, i, 0], s, up)
        fd = remote(high.at[b], far.at[b], agf_s.at[layer, i, 1], agf_r.at[layer, i, 1], s, dn)
        ua.wait_recv()
        fu.start()
        db.wait_recv()
        fd.start()
        sends.extend([fu, fd])
        return fu, fd

    def project(layer, k, c0, c1, first):
        start = blocks[k] * cw + c0
        x = st[layer, k, :, c0:c1].astype(F32)
        rows = pl.ds(pl.multiple_of(start, 128), c1 - c0)
        gain = gain_v[pl.ds(layer, 1), rows]
        xg = (x * gain).astype(BF16)
        for i, w in enumerate((wk, wv, wq)):
            y = dot(xg, w[layer, rows, :])
            if first:
                acc[i] = y
            else:
                acc[i] += y
        return jnp.sum(x * x, axis=1, keepdims=True)

    for layer in range(LAYERS):
        last = layer == LAYERS - 1
        if layer == 0:
            regions = [(0, t_len, f0, f1) for f0, f1 in f_cuts]
            copies, passed = [], []
            square = jnp.zeros((t_len, 1), F32)
            for i, region in enumerate(regions):
                cols = pl.ds(region[2], region[3] - region[2])
                came = pk_recv.at[pl.ds(1, n_chip - 1), :, cols]
                pltpu.make_async_copy(came, came, pk_r.at[i]).wait()
                packed = pk_recv[:, :, cols].reshape(n_chip * slots, region[3] - region[2])
                st[0, 0, :, cols] = dot(unpack, packed).astype(BF16)
                copies.append(share(layer, i, region))
                if i == 0:
                    for w in range(3):
                        weights[layer, w].wait()
                square += project(layer, 0, *region[2:], i == 0)
            passed = [pass_on(layer, i, region, copies[i]) for i, region in enumerate(regions)]
            for i, region in enumerate(regions):
                ua, da, ub, db = copies[i]
                ub.wait_recv()
                square += project(layer, 1, *region[2:], False)
                da.wait_recv()
                square += project(layer, 2, *region[2:], False)
                for c in passed[i]:
                    c.wait_recv()
                square += project(layer, 3, *region[2:], False)
        else:
            for w in range(3):
                weights[layer, w].wait()
            square = project(layer, 0, 0, cw, True)
            passed = [pass_on(layer, i, region, copies[i]) for i, region in enumerate(regions)]
            for ua, da, ub, db in copies:
                ub.wait_recv()
            square += project(layer, 1, 0, cw, False)
            for ua, da, ub, db in copies:
                da.wait_recv()
            square += project(layer, 2, 0, cw, False)
            for pair in passed:
                for c in pair:
                    c.wait_recv()
            square += project(layer, 3, 0, cw, False)
        scale = lax.rsqrt(square * (1.0 / (4 * cw)) + EPSILON)

        kv_copies = [
            remote(kv_own.at[layer, i], kv_past.at[layer, i], kv_s.at[layer, i], kv_r.at[layer, i], nxt, h)
            for i in range(2)
        ]

        def send_on(i):
            @pl.when(s < n_seg - 1)
            def _():
                kv_copies[i].start()

        kv_own[layer, 0] = rope(acc[0], scale).astype(BF16)
        send_on(0)
        kv_own[layer, 1] = (acc[1] * scale).astype(BF16)
        send_on(1)
        q_own[...] = (rope(acc[2], scale) * HD ** (-0.5)).astype(BF16)

        def queries_of(j):
            q = q_own[:, j:j + 128]
            none = jnp.zeros_like(q)
            return jnp.concatenate([jnp.where(head_a, q, none), jnp.where(head_a, none, q)], axis=0)

        for i, j in enumerate(range(0, hw, 128)):
            scores = dot_nt(queries_of(j), kv_own[layer, 0, :, j:j + 128])
            scores = jnp.where(causal2, scores, -1e30)
            top = jnp.max(scores, axis=1, keepdims=True)
            e = jnp.exp(scores - top).astype(BF16)
            values = jnp.concatenate([kv_own[layer, 1, :, j:j + 128], ones], axis=1)
            o_part[i] = dot(e, values)
            mx_part[i] = jnp.broadcast_to(top, (2 * t_len, 128))

        @pl.when(s > 0)
        def _():
            kv_copies[0].wait_recv()
            kv_copies[1].wait_recv()

        for i, j in enumerate(range(0, hw, 128)):
            scores = dot_nt(queries_of(j), kv_past[layer, 0, :, j:j + 128])
            scores = jnp.where(s > 0, scores, -1e30)
            old = mx_part[i]
            top = jnp.maximum(old, jnp.max(scores, axis=1, keepdims=True))
            e = jnp.exp(scores - top).astype(BF16)
            keep = jnp.exp(old - top)
            values = jnp.concatenate([kv_past[layer, 1, :, j:j + 128], ones], axis=1)
            o = dot(e, values)
            num = o_part[i, :, :128] * keep + o[:, :128]
            den = o_part[i, :, 128:] * keep + o[:, 128:]
            m = num / den
            mixed[:, j:j + 128] = jnp.where(head_a, m[:t_len], m[t_len:]).astype(BF16)

        weights[layer, 3].wait()
        part, comb, frecv, rrecv = (
            (part1, comb1, frecv1, rrecv1) if last else (part0, comb0, frecv0, rrecv0)
        )
        n_row, n_col = part.shape[1:]
        if last:
            regions = [(0, n_row, 0, n_col // 2), (0, n_row, n_col // 2, n_col)]
        else:
            regions = [(0, n_row // 2, 0, n_col), (n_row // 2, n_row, 0, n_col)]

        def send(i, k, src, dst, to):
            c = remote(src, dst, rs_s.at[layer, i, k], rs_r.at[layer, i, k], s, to)
            c.start()
            sends.append(c)
            return c

        def far(i):
            a, b = halves(regions[i])
            return (
                send(i, 0, part.at[opp].at[a], frecv.at[0].at[a], up),
                send(i, 1, part.at[opp].at[b], frecv.at[1].at[b], dn),
            )

        def near(i):
            a, b = halves(regions[i])
            return (
                send(i, 2, part.at[up].at[b], rrecv.at[0].at[b], up),
                send(i, 3, part.at[dn].at[a], rrecv.at[1].at[a], dn),
            )

        def join(i, f):
            a, b = halves(regions[i])
            f[0].wait_recv()
            comb[(0,) + a] = (part[(up,) + a].astype(F32) + frecv[(0,) + a].astype(F32)).astype(BF16)
            cu = send(i, 4, comb.at[0].at[a], rrecv.at[0].at[a], up)
            f[1].wait_recv()
            comb[(1,) + b] = (part[(dn,) + b].astype(F32) + frecv[(1,) + b].astype(F32)).astype(BF16)
            return cu, send(i, 5, comb.at[1].at[b], rrecv.at[1].at[b], dn)

        if last:
            fars, nears = [], []
            for b in range(4):
                y = dot(mixed[...], wo[layer, :, b * cw:(b + 1) * cw]).astype(BF16)
                for d in range(4):
                    part[d, :, b * cw:(b + 1) * cw] = y[d * n_row:(d + 1) * n_row]
                if b % 2 == 1:
                    fars.append(far(b // 2))
                    nears.append(near(b // 2))
        else:
            for b in (opp, up, dn, h):
                y = dot(mixed[...], wo[layer, :, pl.ds(pl.multiple_of(b * cw, 128), cw)])
                part[b] = y.astype(BF16)
                if b is opp:
                    fars = [far(0), far(1)]
                if b is dn:
                    nears = [near(0), near(1)]
        joined = [join(i, fars[i]) for i in range(2)]
        copies = []
        for i, region in enumerate(regions):
            for c in nears[i] + joined[i]:
                c.wait_recv()
            r0, r1, c0, c1 = region
            at = (slice(r0, r1), slice(c0, c1))
            total = part[(h,) + at].astype(F32) + rrecv[(0,) + at].astype(F32) + rrecv[(1,) + at].astype(F32)
            if last:
                rows = pl.ds(pl.multiple_of(h * n_row, n_row), n_row)
                if i == 0:
                    for k in range(4):
                        cols = pl.ds(pl.multiple_of(blocks[k] * cw, 128), cw)
                        out_ref[:, cols] = st[layer, k, rows, :].astype(F32)
                out_ref[at] += total
            else:
                st[(layer + 1, 0) + at] = (st[(layer, 0) + at].astype(F32) + total).astype(BF16)
                copies.append(share(layer + 1, i, region))

        @pl.when(s < n_seg - 1)
        def _():
            for c in kv_copies:
                c.wait_send()

    flag_copy.wait()
    flag_ref[0, 0] = jnp.max(jnp.maximum(flag_send[...], flag_recv[...]))
    tab_copy.wait_send()
    others = req_send.at[pl.ds(0, n_chip - 1)]
    pltpu.make_async_copy(others, others, req_s.at[0]).wait()
    for f, (f0, f1) in enumerate(f_cuts):
        others = pk_send.at[pl.ds(1, n_chip - 1), :, pl.ds(f0, f1 - f0)]
        pltpu.make_async_copy(others, others, pk_s.at[f]).wait()
    for c in sends:
        c.wait_send()


def rotary_tables(n_seg, t_len):
    freq = 10000.0 ** (-np.arange(HD // 2, dtype=np.float64) / (HD // 2))
    freq = np.tile(freq, 128 // (HD // 2))[None]
    local = np.arange(t_len, dtype=np.float64)[:, None] * freq
    start = (np.arange(n_seg, dtype=np.float64) * t_len)[:, None] * freq
    both = lambda a: np.stack([np.cos(a), np.sin(a)]).astype(np.float32)
    return both(local), both(start)


def run(slots, n_seg, token_ids, embed_table, norm_gains, query_weight, key_weight, value_weight, out_weight):
    t_len = token_ids.shape[0]
    vr, cw = embed_table.shape
    hw = query_weight.shape[2]
    n_chip = n_seg // 2
    rope_t, rope_s = rotary_tables(n_seg, t_len)
    f_cuts = [(0, 384), (384, cw)] if cw > 384 else [(0, cw)]
    n_cut = max(2, len(f_cuts))
    rows = t_len // 4
    vmem = pltpu.VMEM
    dma = pltpu.SemaphoreType.DMA
    any_spec = pl.BlockSpec(memory_space=pl.ANY)
    vmem_spec = pl.BlockSpec(memory_space=pltpu.VMEM)
    return pl.pallas_call(
        functools.partial(kernel, slots, n_seg, vr, t_len, cw, hw, f_cuts),
        out_shape=(
            jax.ShapeDtypeStruct((rows, 4 * cw), F32),
            jax.ShapeDtypeStruct((1, 1), I32),
        ),
        in_specs=[any_spec] * 9,
        out_specs=(vmem_spec, pl.BlockSpec(memory_space=pltpu.SMEM)),
        scratch_shapes=[
            vmem((1, t_len), I32),
            vmem(norm_gains.shape, F32),
            vmem(rope_t.shape, F32),
            vmem(rope_s.shape, F32),
            vmem((2, vr, cw), BF16),
            vmem(query_weight.shape, BF16),
            vmem(key_weight.shape, BF16),
            vmem(value_weight.shape, BF16),
            vmem(out_weight.shape, BF16),
            vmem((n_chip, 1, t_len), I32),
            vmem((n_chip, 1, t_len), I32),
            vmem((8, t_len), I32),
            vmem((8, t_len), I32),
            vmem((2, n_chip * slots, vr), BF16),
            vmem((n_chip, slots, cw), BF16),
            vmem((n_chip, slots, cw), BF16),
            vmem((LAYERS, 4, t_len, cw), BF16),
            vmem((3, t_len, hw), F32),
            vmem((LAYERS, 2, t_len, hw), BF16),
            vmem((LAYERS, 2, t_len, hw), BF16),
            vmem((t_len, hw), BF16),
            vmem((hw // 128, 2 * t_len, 256), F32),
            vmem((hw // 128, 2 * t_len, 128), F32),
            vmem((t_len, hw), BF16),
            vmem((4, t_len, cw), BF16),
            vmem((4, rows, 4 * cw), BF16),
            vmem((2, t_len, cw), BF16),
            vmem((2, rows, 4 * cw), BF16),
            vmem((2, t_len, cw), BF16),
            vmem((2, rows, 4 * cw), BF16),
            vmem((2, t_len, cw), BF16),
            vmem((2, rows, 4 * cw), BF16),
            dma((5,)),
            dma((LAYERS, 4)),
            dma((2,)),
            dma((1,)),
            dma((n_chip,)),
            dma((2,)),
            dma((n_cut,)),
            dma((n_cut,)),
            dma((LAYERS, n_cut, 2, 2)),
            dma((LAYERS, n_cut, 2, 2)),
            dma((LAYERS, n_cut, 2)),
            dma((LAYERS, n_cut, 2)),
            dma((LAYERS, 2)),
            dma((LAYERS, 2)),
            dma((LAYERS, 2, 6)),
            dma((LAYERS, 2, 6)),
        ],
        compiler_params=pltpu.CompilerParams(
            collective_id=int(slots == ALL_SLOTS), has_side_effects=True, vmem_limit_bytes=56 * 2 ** 20
        ),
        name="decoder",
    )(
        token_ids.reshape(1, t_len), embed_table, norm_gains,
        query_weight, key_weight, value_weight, out_weight,
        jnp.asarray(rope_t), jnp.asarray(rope_s),
    )


def body(n_seg, *arrays):
    out, flag = run(SLOTS, n_seg, *arrays)
    return lax.cond(
        flag[0, 0] > 0,
        lambda: run(ALL_SLOTS, n_seg, *arrays)[0].astype(BF16),
        lambda: out.astype(BF16),
    )


def solution(mesh):
    placed = (
        P("seg"),
        P("seg", "head"),
        P(),
        P(None, None, "head"),
        P(None, None, "head"),
        P(None, None, "head"),
        P(None, "head", None),
    )
    return jax.shard_map(
        functools.partial(body, mesh.shape["seg"]),
        mesh=mesh, in_specs=placed, out_specs=P(("seg", "head"), None), check_vma=False,
    )
```

time: 72.1 us -> 65 us (0.902)
  Pallas kernels: 70 us -> 62.4 us
    pallas_call x1, Pallas kernels: 70 us -> 62.4 us  [run(): pl.pallas_call(functools.partial(kernel, slots, n_seg, vr, t_len, cw, hw,...]
where the time goes in v3:
time: 65 us; the launch traced here: 64 us
  Pallas kernels  62.4 us (96%)
  between operations  0.7 us (1%)
  other arithmetic  0.68 us (1%)
    pallas_call x1, Pallas kernels, run(): pl.pallas_call(functools.partial(kernel, slots, n_seg, vr, t_len, cw, hw,...  62.4 us

profile of v3, /device:TPU:0, one launch (start us, length us, event | category | flops | bytes accessed | tf_op | source)
XLA Modules:
  0.0 64.0 jit_solution(13772078143135852341)
XLA Ops:
  0.0 0.0 copy-start
  0.0 0.0 copy-start.1
  0.0 0.0 copy-start.2
  0.0 0.0 copy-start.3
  0.0 0.0 copy-start.4
  0.0 0.0 copy-start.5
  0.0 62.4 %decoder.3 = (f32[32,2560]{1,0:T(8,128)S(1)}, s32[1,1]{1,0:T(1,128)}) custom-call(s32[1,128]{1,0:T(1,128)} %bitcast.3, bf16[1000,640]{1,0:T(8,128)(2,1)} %tab_hbm.1, f32[2,2560]{1,0:T(2,128)} %gain_hbm.1, bf16[2,2560,512]{2,1,0:T(8,128)(2,1)} %wq_hbm.1, bf16[2,2560,512]{2,1,0:T(8,128)(2,1)} %wk_hbm.1, bf16[2,2560,512]{2,1,0:T(8,128)(2,1)} %wv_hbm.1, ...), custom_call_target="tpu_custom_call" | custom-call | tf_op jit(solution)/shard_map/decoder/pallas_call | solution.py:468
  63.0 0.0 copy-done
  63.1 0.0 copy-done.1
  63.1 0.0 copy-done.2
  63.1 0.0 copy-done.3
  63.1 0.0 copy-done.4
  63.1 0.0 copy-done.5
  63.1 0.2 conditional.6
  63.3 0.7 %convert_element_type.21 = bf16[32,2560]{1,0:T(8,128)(2,1)} convert(f32[32,2560]{1,0:T(8,128)S(1)} %get-tuple-element.51) | non-fusion elementwise | flops 81920 | bytes 491520 | tf_op jit(solution)/shard_map/cond/branch_0_fun/convert_element_type | solution.py:542
Async XLA Ops:
  0.0 63.0 %copy-start = (bf16[2,2560,512]{2,1,0:T(8,128)(2,1)S(1)}, bf16[2,2560,512]{2,1,0:T(8,128)(2,1)}, u32[]{:S(2)}) copy-start(bf16[2,2560,512]{2,1,0:T(8,128)(2,1)} %wq_hbm.1) | copy-start | bytes 15728644
  0.0 63.1 %copy-start.1 = (bf16[1000,640]{1,0:T(8,128)(2,1)S(1)}, bf16[1000,640]{1,0:T(8,128)(2,1)}, u32[]{:S(2)}) copy-start(bf16[1000,640]{1,0:T(8,128)(2,1)} %tab_hbm.1) | copy-start | bytes 3840004
  0.0 63.1 %copy-start.2 = (f32[2,128,128]{2,1,0:T(8,128)S(1)}, f32[2,128,128]{2,1,0:T(8,128)}, u32[]{:S(2)}) copy-start(f32[2,128,128]{2,1,0:T(8,128)} %constant.7.clone.rope_t_hbm) | copy-start | bytes 393220
  0.0 63.1 %copy-start.3 = (f32[2,32,128]{2,1,0:T(8,128)S(1)}, f32[2,32,128]{2,1,0:T(8,128)}, u32[]{:S(2)}) copy-start(f32[2,32,128]{2,1,0:T(8,128)} %constant.8.clone.rope_s_hbm) | copy-start | bytes 98308
  0.0 63.1 %copy-start.4 = (f32[2,2560]{1,0:T(2,128)S(1)}, f32[2,2560]{1,0:T(2,128)}, u32[]{:S(2)}) copy-start(f32[2,2560]{1,0:T(2,128)} %gain_hbm.1) | copy-start | bytes 61444
  0.0 63.1 %copy-start.5 = (s32[128]{0:T(128)S(1)}, s32[128]{0:T(128)}, u32[]{:S(2)}) copy-start(s32[128]{0:T(128)} %param.13) | copy-start | bytes 1540

commit v4 on v3

--- a/solution.py
+++ b/solution.py
@@ -75,6 +75,7 @@
         hello(2 * chip_at(dx, dz) + core, h)
     for other in (up, dn):
         hello(s, other)
+    hello(s, opp)
     hello(sib, h)
     hello(prv, h)
 
@@ -91,7 +92,7 @@
     for layer in range(LAYERS):
         for i, (a, b) in enumerate([(wk_hbm, wk), (wv_hbm, wv), (wq_hbm, wq), (wo_hbm, wo)]):
             c = pltpu.make_async_copy(a.at[layer], b.at[layer], w_sem.at[layer, i])
-            c.start()
+            c.start(priority=1)
             weights[layer, i] = c
 
     loads[0].wait()
@@ -135,7 +136,7 @@
     def _():
         kv_past[...] = jnp.zeros_like(kv_past)
 
-    pl.semaphore_wait(bar, 2 + 2 + n_chip - 1)
+    pl.semaphore_wait(bar, 3 + 2 + n_chip - 1)
 
     group = min(4, n_chip)
     group_of = {o[0]: i // group for i, o in enumerate(offsets)}
@@ -216,6 +217,9 @@
         mid, cols = (r0 + r1) // 2, pl.ds(c0, c1 - c0)
         return (pl.ds(r0, mid - r0), cols), (pl.ds(mid, r1 - mid), cols)
 
+    def straight(layer, i):
+        return layer == 1 and i == 1
+
     def share(layer, i, region):
         a, b = halves(region)
         own, low, high = st.at[layer, 0], st.at[layer, 1], st.at[layer, 2]
@@ -229,9 +233,21 @@
         for c in (ua, db, ub, da):
             c.start()
         sends.extend([ua, db, ub, da])
+        if straight(layer, i):
+            whole = (pl.ds(region[0], region[1] - region[0]), b[1])
+            c = remote(
+                own.at[whole], st.at[layer, 3].at[whole], agf_s.at[layer, i, 0], agf_r.at[layer, i, 0], s, opp
+            )
+            c.start()
+            sends.append(c)
+            return ua, da, ub, db, c
         return ua, da, ub, db
 
     def pass_on(layer, i, region, copies):
+        if straight(layer, i):
+            copies[0].wait_recv()
+            copies[3].wait_recv()
+            return copies[4:]
         ua, da, ub, db = copies
         a, b = halves(region)
         low, high, far = st.at[layer, 1], st.at[layer, 2], st.at[layer, 3]
@@ -244,14 +260,14 @@
         sends.extend([fu, fd])
         return fu, fd
 
-    def project(layer, k, c0, c1, first):
+    def project(layer, k, c0, c1, first, which=(0, 1, 2)):
         start = blocks[k] * cw + c0
         x = st[layer, k, :, c0:c1].astype(F32)
         rows = pl.ds(pl.multiple_of(start, 128), c1 - c0)
         gain = gain_v[pl.ds(layer, 1), rows]
         xg = (x * gain).astype(BF16)
-        for i, w in enumerate((wk, wv, wq)):
-            y = dot(xg, w[layer, rows, :])
+        for i in which:
+            y = dot(xg, (wk, wv, wq)[i][layer, rows, :])
             if first:
                 acc[i] = y
             else:
@@ -277,29 +293,31 @@
                 square += project(layer, 0, *region[2:], i == 0)
             passed = [pass_on(layer, i, region, copies[i]) for i, region in enumerate(regions)]
             for i, region in enumerate(regions):
-                ua, da, ub, db = copies[i]
+                ua, da, ub, db = copies[i][:4]
                 ub.wait_recv()
                 square += project(layer, 1, *region[2:], False)
                 da.wait_recv()
                 square += project(layer, 2, *region[2:], False)
                 for c in passed[i]:
                     c.wait_recv()
-                square += project(layer, 3, *region[2:], False)
+                final = (layer, 3, *region[2:], False)
+                square += project(*final, (0, 1) if i == len(regions) - 1 else (0, 1, 2))
         else:
             for w in range(3):
                 weights[layer, w].wait()
             square = project(layer, 0, 0, cw, True)
             passed = [pass_on(layer, i, region, copies[i]) for i, region in enumerate(regions)]
-            for ua, da, ub, db in copies:
+            for ua, da, ub, db, *_ in copies:
                 ub.wait_recv()
             square += project(layer, 1, 0, cw, False)
-            for ua, da, ub, db in copies:
+            for ua, da, ub, db, *_ in copies:
                 da.wait_recv()
             square += project(layer, 2, 0, cw, False)
             for pair in passed:
                 for c in pair:
                     c.wait_recv()
-            square += project(layer, 3, 0, cw, False)
+            final = (layer, 3, 0, cw, False)
+            square += project(*final, (0, 1))
         scale = lax.rsqrt(square * (1.0 / (4 * cw)) + EPSILON)
 
         kv_copies = [
@@ -316,6 +334,7 @@
         send_on(0)
         kv_own[layer, 1] = (acc[1] * scale).astype(BF16)
         send_on(1)
+        project(*final, (2,))
         q_own[...] = (rope(acc[2], scale) * HD ** (-0.5)).astype(BF16)
 
         def queries_of(j):
@@ -391,14 +410,14 @@
             return cu, send(i, 5, comb.at[1].at[b], rrecv.at[1].at[b], dn)
 
         if last:
-            fars, nears = [], []
+            fars = []
             for b in range(4):
                 y = dot(mixed[...], wo[layer, :, b * cw:(b + 1) * cw]).astype(BF16)
                 for d in range(4):
                     part[d, :, b * cw:(b + 1) * cw] = y[d * n_row:(d + 1) * n_row]
                 if b % 2 == 1:
                     fars.append(far(b // 2))
-                    nears.append(near(b // 2))
+            nears = [near(0), near(1)]
         else:
             for b in (opp, up, dn, h):
                 y = dot(mixed[...], wo[layer, :, pl.ds(pl.multiple_of(b * cw, 128), cw)])

time: 65 us -> 63.3 us (0.974)
  Pallas kernels: 62.4 us -> 60.6 us
    pallas_call x1, Pallas kernels: 62.4 us -> 60.6 us  [run(): pl.pallas_call(functools.partial(kernel, slots, n_seg, vr, t_len, cw, hw,...]
where the time goes in v4:
time: 63.3 us; the launch traced here: 62.3 us
  Pallas kernels  60.6 us (96%)
  between operations  0.7 us (1%)
  other arithmetic  0.68 us (1%)
    pallas_call x1, Pallas kernels, run(): pl.pallas_call(functools.partial(kernel, slots, n_seg, vr, t_len, cw, hw,...  60.6 us

profile of v4, /device:TPU:0, one launch (start us, length us, event | category | flops | bytes accessed | tf_op | source)
XLA Modules:
  0.0 62.3 jit_solution(2820340335218551861)
XLA Ops:
  0.0 0.0 copy-start
  0.0 0.0 copy-start.1
  0.0 0.0 copy-start.2
  0.0 0.0 copy-start.3
  0.0 0.0 copy-start.4
  0.0 0.0 copy-start.5
  0.0 60.6 %decoder.3 = (f32[32,2560]{1,0:T(8,128)S(1)}, s32[1,1]{1,0:T(1,128)}) custom-call(s32[1,128]{1,0:T(1,128)} %bitcast.3, bf16[1000,640]{1,0:T(8,128)(2,1)} %tab_hbm.1, f32[2,2560]{1,0:T(2,128)} %gain_hbm.1, bf16[2,2560,512]{2,1,0:T(8,128)(2,1)} %wq_hbm.1, bf16[2,2560,512]{2,1,0:T(8,128)(2,1)} %wk_hbm.1, bf16[2,2560,512]{2,1,0:T(8,128)(2,1)} %wv_hbm.1, ...), custom_call_target="tpu_custom_call" | custom-call | tf_op jit(solution)/shard_map/decoder/pallas_call | solution.py:487
  61.3 0.0 copy-done
  61.3 0.0 copy-done.1
  61.3 0.0 copy-done.2
  61.3 0.0 copy-done.3
  61.3 0.0 copy-done.4
  61.3 0.0 copy-done.5
  61.3 0.2 conditional.6
  61.6 0.7 %convert_element_type.21 = bf16[32,2560]{1,0:T(8,128)(2,1)} convert(f32[32,2560]{1,0:T(8,128)S(1)} %get-tuple-element.51) | non-fusion elementwise | flops 81920 | bytes 491520 | tf_op jit(solution)/shard_map/cond/branch_0_fun/convert_element_type | solution.py:561
Async XLA Ops:
  0.0 61.3 %copy-start = (bf16[2,2560,512]{2,1,0:T(8,128)(2,1)S(1)}, bf16[2,2560,512]{2,1,0:T(8,128)(2,1)}, u32[]{:S(2)}) copy-start(bf16[2,2560,512]{2,1,0:T(8,128)(2,1)} %wq_hbm.1) | copy-start | bytes 15728644
  0.0 61.3 %copy-start.1 = (bf16[1000,640]{1,0:T(8,128)(2,1)S(1)}, bf16[1000,640]{1,0:T(8,128)(2,1)}, u32[]{:S(2)}) copy-start(bf16[1000,640]{1,0:T(8,128)(2,1)} %tab_hbm.1) | copy-start | bytes 3840004
  0.0 61.3 %copy-start.2 = (f32[2,128,128]{2,1,0:T(8,128)S(1)}, f32[2,128,128]{2,1,0:T(8,128)}, u32[]{:S(2)}) copy-start(f32[2,128,128]{2,1,0:T(8,128)} %constant.7.clone.rope_t_hbm) | copy-start | bytes 393220
  0.0 61.3 %copy-start.3 = (f32[2,32,128]{2,1,0:T(8,128)S(1)}, f32[2,32,128]{2,1,0:T(8,128)}, u32[]{:S(2)}) copy-start(f32[2,32,128]{2,1,0:T(8,128)} %constant.8.clone.rope_s_hbm) | copy-start | bytes 98308
  0.0 61.3 %copy-start.4 = (f32[2,2560]{1,0:T(2,128)S(1)}, f32[2,2560]{1,0:T(2,128)}, u32[]{:S(2)}) copy-start(f32[2,2560]{1,0:T(2,128)} %gain_hbm.1) | copy-start | bytes 61444
  0.0 61.3 %copy-start.5 = (s32[128]{0:T(128)S(1)}, s32[128]{0:T(128)}, u32[]{:S(2)}) copy-start(s32[128]{0:T(128)} %param.13) | copy-start | bytes 1540

commit v5 on v4

--- a/solution.py
+++ b/solution.py
@@ -124,13 +124,6 @@
         row = jnp.sum(row, axis=0, keepdims=True) - 1
         req_send[slot] = jnp.where(lane_row == t_len - 1, full, row) if slots < t_len else row
     req_recv[0] = req_send[0]
-
-    px = sum(jnp.where(pc >= i * nz, one, zero) for i in range(1, nx)) if nx > 1 else jnp.zeros_like(pc)
-    rx, rz = px - x, pc - px * nz - z
-    rel = jnp.where(rx < 0, rx + nx, rx) * nz + jnp.where(rz < 0, rz + nz, rz)
-    slot_key = rel[:, 0:1] * slots + rank_col
-    slots_iota = lax.broadcasted_iota(I32, (t_len, n_chip * slots), 1)
-    unpack = jnp.where(jnp.broadcast_to(slot_key, slots_iota.shape) == slots_iota, 1.0, 0.0).astype(BF16)
 
     @pl.when(s == 0)
     def _():
@@ -188,6 +181,13 @@
     flag_copy = remote(flag_send, flag_recv, flag_sem.at[0], flag_sem.at[1], sib, h)
     flag_copy.start()
 
+    px = sum(jnp.where(pc >= i * nz, one, zero) for i in range(1, nx)) if nx > 1 else jnp.zeros_like(pc)
+    rx, rz = px - x, pc - px * nz - z
+    rel = jnp.where(rx < 0, rx + nx, rx) * nz + jnp.where(rz < 0, rz + nz, rz)
+    slot_key = rel[:, 0:1] * slots + rank_col
+    slots_iota = lax.broadcasted_iota(I32, (t_len, n_chip * slots), 1)
+    unpack = jnp.where(jnp.broadcast_to(slot_key, slots_iota.shape) == slots_iota, 1.0, 0.0).astype(BF16)
+
     for c in loads[2:]:
         c.wait()
     cos_t, sin_t = rope_t[0], rope_t[1]
@@ -200,7 +200,7 @@
 
     def rope(x, scale):
         pieces = []
-        for j in range(0, hw, 128):
+        for j in range(0, x.shape[1], 128):
             y = x[:, j:j + 128] * scale
             partner = jnp.where(front, pltpu.roll(y, 128 - HD // 2, 1), pltpu.roll(y, HD // 2, 1))
             pieces.append(y * cosine + partner * sine)
@@ -320,9 +320,13 @@
             square += project(*final, (0, 1))
         scale = lax.rsqrt(square * (1.0 / (4 * cw)) + EPSILON)
 
+        pairs = max(1, hw // 256)
         kv_copies = [
-            remote(kv_own.at[layer, i], kv_past.at[layer, i], kv_s.at[layer, i], kv_r.at[layer, i], nxt, h)
-            for i in range(2)
+            remote(
+                kv_own.at[layer, pl.ds(i, pairs)], kv_past.at[layer, pl.ds(i, pairs)],
+                kv_s.at[layer, i], kv_r.at[layer, i], nxt, h,
+            )
+            for i in range(0, hw // 128, pairs)
         ]
 
         def send_on(i):
@@ -330,10 +334,12 @@
             def _():
                 kv_copies[i].start()
 
-        kv_own[layer, 0] = rope(acc[0], scale).astype(BF16)
-        send_on(0)
-        kv_own[layer, 1] = (acc[1] * scale).astype(BF16)
-        send_on(1)
+        for i in range(hw // 128):
+            cols = slice(i * 128, (i + 1) * 128)
+            kv_own[layer, i, 0] = rope(acc[0, :, cols], scale).astype(BF16)
+            kv_own[layer, i, 1] = (acc[1, :, cols] * scale).astype(BF16)
+            if (i + 1) % pairs == 0:
+                send_on(i // pairs)
         project(*final, (2,))
         q_own[...] = (rope(acc[2], scale) * HD ** (-0.5)).astype(BF16)
 
@@ -343,27 +349,24 @@
             return jnp.concatenate([jnp.where(head_a, q, none), jnp.where(head_a, none, q)], axis=0)
 
         for i, j in enumerate(range(0, hw, 128)):
-            scores = dot_nt(queries_of(j), kv_own[layer, 0, :, j:j + 128])
+            scores = dot_nt(queries_of(j), kv_own[layer, i, 0])
             scores = jnp.where(causal2, scores, -1e30)
             top = jnp.max(scores, axis=1, keepdims=True)
             e = jnp.exp(scores - top).astype(BF16)
-            values = jnp.concatenate([kv_own[layer, 1, :, j:j + 128], ones], axis=1)
+            values = jnp.concatenate([kv_own[layer, i, 1], ones], axis=1)
             o_part[i] = dot(e, values)
             mx_part[i] = jnp.broadcast_to(top, (2 * t_len, 128))
 
-        @pl.when(s > 0)
-        def _():
-            kv_copies[0].wait_recv()
-            kv_copies[1].wait_recv()
-
         for i, j in enumerate(range(0, hw, 128)):
-            scores = dot_nt(queries_of(j), kv_past[layer, 0, :, j:j + 128])
+            if i % pairs == 0:
+                pl.when(s > 0)(kv_copies[i // pairs].wait_recv)
+            scores = dot_nt(queries_of(j), kv_past[layer, i, 0])
             scores = jnp.where(s > 0, scores, -1e30)
             old = mx_part[i]
             top = jnp.maximum(old, jnp.max(scores, axis=1, keepdims=True))
             e = jnp.exp(scores - top).astype(BF16)
             keep = jnp.exp(old - top)
-            values = jnp.concatenate([kv_past[layer, 1, :, j:j + 128], ones], axis=1)
+            values = jnp.concatenate([kv_past[layer, i, 1], ones], axis=1)
             o = dot(e, values)
             num = o_part[i, :, :128] * keep + o[:, :128]
             den = o_part[i, :, 128:] * keep + o[:, 128:]
@@ -511,8 +514,8 @@
             vmem((n_chip, slots, cw), BF16),
             vmem((LAYERS, 4, t_len, cw), BF16),
             vmem((3, t_len, hw), F32),
-            vmem((LAYERS, 2, t_len, hw), BF16),
-            vmem((LAYERS, 2, t_len, hw), BF16),
+            vmem((LAYERS, hw // 128, 2, t_len, 128), BF16),
+            vmem((LAYERS, hw // 128, 2, t_len, 128), BF16),
             vmem((t_len, hw), BF16),
             vmem((hw // 128, 2 * t_len, 256), F32),
             vmem((hw // 128, 2 * t_len, 128), F32),
@@ -537,8 +540,8 @@
             dma((LAYERS, n_cut, 2, 2)),
             dma((LAYERS, n_cut, 2)),
             dma((LAYERS, n_cut, 2)),
-            dma((LAYERS, 2)),
-            dma((LAYERS, 2)),
+            dma((LAYERS, hw // 128)),
+            dma((LAYERS, hw // 128)),
             dma((LAYERS, 2, 6)),
             dma((LAYERS, 2, 6)),
         ],

time: 63.3 us -> 62.9 us (level)
  no operation moved by 1% of the time
where the time goes in v5:
time: 62.9 us; the launch traced here: 61.9 us
  Pallas kernels  60.3 us (96%)
  between operations  0.7 us (1%)
  other arithmetic  0.68 us (1%)
    pallas_call x1, Pallas kernels, run(): pl.pallas_call(functools.partial(kernel, slots, n_seg, vr, t_len, cw, hw,...  60.3 us

profile of v5, /device:TPU:0, one launch (start us, length us, event | category | flops | bytes accessed | tf_op | source)
XLA Modules:
  0.0 61.9 jit_solution(6225519761857622917)
XLA Ops:
  0.0 0.0 copy-start
  0.0 0.0 copy-start.1
  0.0 0.0 copy-start.2
  0.0 0.0 copy-start.3
  0.0 0.0 copy-start.4
  0.0 0.0 copy-start.5
  0.0 60.3 %decoder.3 = (f32[32,2560]{1,0:T(8,128)S(1)}, s32[1,1]{1,0:T(1,128)}) custom-call(s32[1,128]{1,0:T(1,128)} %bitcast.3, bf16[1000,640]{1,0:T(8,128)(2,1)} %tab_hbm.1, f32[2,2560]{1,0:T(2,128)} %gain_hbm.1, bf16[2,2560,512]{2,1,0:T(8,128)(2,1)} %wq_hbm.1, bf16[2,2560,512]{2,1,0:T(8,128)(2,1)} %wk_hbm.1, bf16[2,2560,512]{2,1,0:T(8,128)(2,1)} %wv_hbm.1, ...), custom_call_target="tpu_custom_call" | custom-call | tf_op jit(solution)/shard_map/decoder/pallas_call | solution.py:490
  61.0 0.0 copy-done
  61.0 0.0 copy-done.1
  61.0 0.0 copy-done.2
  61.0 0.0 copy-done.3
  61.0 0.0 copy-done.4
  61.0 0.0 copy-done.5
  61.0 0.2 conditional.6
  61.3 0.7 %convert_element_type.21 = bf16[32,2560]{1,0:T(8,128)(2,1)} convert(f32[32,2560]{1,0:T(8,128)S(1)} %get-tuple-element.51) | non-fusion elementwise | flops 81920 | bytes 491520 | tf_op jit(solution)/shard_map/cond/branch_0_fun/convert_element_type | solution.py:564
Async XLA Ops:
  0.0 61.0 %copy-start = (bf16[2,2560,512]{2,1,0:T(8,128)(2,1)S(1)}, bf16[2,2560,512]{2,1,0:T(8,128)(2,1)}, u32[]{:S(2)}) copy-start(bf16[2,2560,512]{2,1,0:T(8,128)(2,1)} %wq_hbm.1) | copy-start | bytes 15728644
  0.0 61.0 %copy-start.1 = (bf16[1000,640]{1,0:T(8,128)(2,1)S(1)}, bf16[1000,640]{1,0:T(8,128)(2,1)}, u32[]{:S(2)}) copy-start(bf16[1000,640]{1,0:T(8,128)(2,1)} %tab_hbm.1) | copy-start | bytes 3840004
  0.0 61.0 %copy-start.2 = (f32[2,128,128]{2,1,0:T(8,128)S(1)}, f32[2,128,128]{2,1,0:T(8,128)}, u32[]{:S(2)}) copy-start(f32[2,128,128]{2,1,0:T(8,128)} %constant.7.clone.rope_t_hbm) | copy-start | bytes 393220
  0.0 61.0 %copy-start.3 = (f32[2,32,128]{2,1,0:T(8,128)S(1)}, f32[2,32,128]{2,1,0:T(8,128)}, u32[]{:S(2)}) copy-start(f32[2,32,128]{2,1,0:T(8,128)} %constant.8.clone.rope_s_hbm) | copy-start | bytes 98308
  0.0 61.0 %copy-start.4 = (f32[2,2560]{1,0:T(2,128)S(1)}, f32[2,2560]{1,0:T(2,128)}, u32[]{:S(2)}) copy-start(f32[2,2560]{1,0:T(2,128)} %gain_hbm.1) | copy-start | bytes 61444
  0.0 61.0 %copy-start.5 = (s32[128]{0:T(128)S(1)}, s32[128]{0:T(128)}, u32[]{:S(2)}) copy-start(s32[128]{0:T(128)} %param.13) | copy-start | bytes 1540

commit v6 on v5

--- a/solution.py
+++ b/solution.py
@@ -406,10 +406,10 @@
         def join(i, f):
             a, b = halves(regions[i])
             f[0].wait_recv()
-            comb[(0,) + a] = (part[(up,) + a].astype(F32) + frecv[(0,) + a].astype(F32)).astype(BF16)
+            comb[(0,) + a] = part[(up,) + a] + frecv[(0,) + a]
             cu = send(i, 4, comb.at[0].at[a], rrecv.at[0].at[a], up)
             f[1].wait_recv()
-            comb[(1,) + b] = (part[(dn,) + b].astype(F32) + frecv[(1,) + b].astype(F32)).astype(BF16)
+            comb[(1,) + b] = part[(dn,) + b] + frecv[(1,) + b]
             return cu, send(i, 5, comb.at[1].at[b], rrecv.at[1].at[b], dn)
 
         if last:

time: 62.9 us -> 62.9 us (level)
  no operation moved by 1% of the time
where the time goes in v6:
time: 62.9 us; the launch traced here: 61.9 us
  Pallas kernels  60.3 us (96%)
  between operations  0.7 us (1%)
  other arithmetic  0.68 us (1%)
    pallas_call x1, Pallas kernels, run(): pl.pallas_call(functools.partial(kernel, slots, n_seg, vr, t_len, cw, hw,...  60.3 us

profile of v6, /device:TPU:0, one launch (start us, length us, event | category | flops | bytes accessed | tf_op | source)
XLA Modules:
  0.0 61.9 jit_solution(6764977171738010124)
XLA Ops:
  0.0 0.0 copy-start
  0.0 0.0 copy-start.1
  0.0 0.0 copy-start.2
  0.0 0.0 copy-start.3
  0.0 0.0 copy-start.4
  0.0 0.0 copy-start.5
  0.0 60.3 %decoder.3 = (f32[32,2560]{1,0:T(8,128)S(1)}, s32[1,1]{1,0:T(1,128)}) custom-call(s32[1,128]{1,0:T(1,128)} %bitcast.3, bf16[1000,640]{1,0:T(8,128)(2,1)} %tab_hbm.1, f32[2,2560]{1,0:T(2,128)} %gain_hbm.1, bf16[2,2560,512]{2,1,0:T(8,128)(2,1)} %wq_hbm.1, bf16[2,2560,512]{2,1,0:T(8,128)(2,1)} %wk_hbm.1, bf16[2,2560,512]{2,1,0:T(8,128)(2,1)} %wv_hbm.1, ...), custom_call_target="tpu_custom_call" | custom-call | tf_op jit(solution)/shard_map/decoder/pallas_call | solution.py:490
  61.0 0.0 copy-done
  61.0 0.0 copy-done.1
  61.0 0.0 copy-done.2
  61.0 0.0 copy-done.3
  61.0 0.0 copy-done.4
  61.0 0.0 copy-done.5
  61.0 0.2 conditional.6
  61.3 0.7 %convert_element_type.21 = bf16[32,2560]{1,0:T(8,128)(2,1)} convert(f32[32,2560]{1,0:T(8,128)S(1)} %get-tuple-element.51) | non-fusion elementwise | flops 81920 | bytes 491520 | tf_op jit(solution)/shard_map/cond/branch_0_fun/convert_element_type | solution.py:564
Async XLA Ops:
  0.0 61.0 %copy-start = (bf16[2,2560,512]{2,1,0:T(8,128)(2,1)S(1)}, bf16[2,2560,512]{2,1,0:T(8,128)(2,1)}, u32[]{:S(2)}) copy-start(bf16[2,2560,512]{2,1,0:T(8,128)(2,1)} %wq_hbm.1) | copy-start | bytes 15728644
  0.0 61.0 %copy-start.1 = (bf16[1000,640]{1,0:T(8,128)(2,1)S(1)}, bf16[1000,640]{1,0:T(8,128)(2,1)}, u32[]{:S(2)}) copy-start(bf16[1000,640]{1,0:T(8,128)(2,1)} %tab_hbm.1) | copy-start | bytes 3840004
  0.0 61.0 %copy-start.2 = (f32[2,128,128]{2,1,0:T(8,128)S(1)}, f32[2,128,128]{2,1,0:T(8,128)}, u32[]{:S(2)}) copy-start(f32[2,128,128]{2,1,0:T(8,128)} %constant.7.clone.rope_t_hbm) | copy-start | bytes 393220
  0.0 61.0 %copy-start.3 = (f32[2,32,128]{2,1,0:T(8,128)S(1)}, f32[2,32,128]{2,1,0:T(8,128)}, u32[]{:S(2)}) copy-start(f32[2,32,128]{2,1,0:T(8,128)} %constant.8.clone.rope_s_hbm) | copy-start | bytes 98308
  0.0 61.0 %copy-start.4 = (f32[2,2560]{1,0:T(2,128)S(1)}, f32[2,2560]{1,0:T(2,128)}, u32[]{:S(2)}) copy-start(f32[2,2560]{1,0:T(2,128)} %gain_hbm.1) | copy-start | bytes 61444
  0.0 61.0 %copy-start.5 = (s32[128]{0:T(128)S(1)}, s32[128]{0:T(128)}, u32[]{:S(2)}) copy-start(s32[128]{0:T(128)} %param.13) | copy-start | bytes 1540
